TPU v7x, 32 devices: a whole 2x2x4 slice. The times are simulated.
32 devices in a mesh: ctx: 16 (over z, x, core), kv: 2 (over y).
Axes of the slice: x: 2, y: 2, z: 4, core: 2. Of those that a mesh axis runs over, the one named last changes fastest.
Arguments:
- queries: bfloat16 [3072, 5120], P('ctx', 'kv'), may hold values from -16 to 16
- keys: bfloat16 [3072, 1024], P('ctx', 'kv'), may hold values from -8 to 8
- values: bfloat16 [3072, 1024], P('ctx', 'kv'), may hold values from -6 to 6
- w_out: bfloat16 [5120, 5120], P('kv', 'ctx'), may hold values from -0.078125 to 0.078125
- grad_y: bfloat16 [3072, 5120], P('ctx', 'kv'), may hold values from -6 to 6
- resp_blocks: int32 [4], replicated, may hold values from 1 to 6, 12 in all
Outputs:
- y_out: bfloat16 [3072, 5120], P('ctx', 'kv')
- grad_q: bfloat16 [3072, 5120], P('ctx', 'kv')
- grad_k: bfloat16 [3072, 1024], P('ctx', 'kv')
- grad_v: bfloat16 [3072, 1024], P('ctx', 'kv')
Inputs may be any that keep to these rules, and one draw needn't show every extreme that they name: resp_blocks sums to 12; the longest response has exactly 6 blocks.
All inputs are finite; a program needn't handle non-finite values.
Results may differ from a plain program's by a relative error of at most 0.035.
Values may be sent and summed in bfloat16 or wider, within the bound.
A program may use at most 128 MiB of HBM per device.

v0:
```python
import math

import jax
import jax.numpy as jnp
from jax import lax
from jax.sharding import PartitionSpec as P

H = 40
KVH = 8
HD = 128
BLK = 128
NRESP = 4


NEG = -1e30


def segment_ids(positions, resp_blocks, prompt_len):
    resp_ends = jnp.cumsum(resp_blocks) * BLK
    offsets = positions - prompt_len
    later = jnp.sum((offsets[:, None] >= resp_ends[None, : NRESP - 1]).astype(jnp.int32), axis=1)
    return jnp.where(positions < prompt_len, 0, 1 + later)


def visible_pairs(query_pos, query_seg, key_pos, key_seg):
    causal = key_pos[None, :] <= query_pos[:, None]
    same = (key_seg[None, :] == 0) | (key_seg[None, :] == query_seg[:, None])
    return causal & same


def local(queries, keys, values, w_out, grad_y, resp_blocks):
    tok_rows = queries.shape[0]
    total_rows = tok_rows * lax.axis_size("ctx")
    prompt_len = total_rows // 2
    group_size = H // KVH
    kv_local = keys.shape[1] // HD
    score_scale = 1.0 / math.sqrt(HD)
    key_block = 4 * BLK
    block_count = total_rows // key_block
    query_pos = lax.axis_index("ctx") * tok_rows + jnp.arange(tok_rows, dtype=jnp.int32)
    query_seg = segment_ids(query_pos, resp_blocks, prompt_len)
    q_four = queries.reshape(tok_rows, kv_local, group_size, HD)
    key_all, value_all = (
        lax.all_gather(keys, "ctx", axis=0, tiled=True),
        lax.all_gather(values, "ctx", axis=0, tiled=True),
    )

    def block_view(block_index):
        first = block_index * key_block
        key_pos = first + jnp.arange(key_block, dtype=jnp.int32)
        key_seg = segment_ids(key_pos, resp_blocks, prompt_len)
        visible = visible_pairs(query_pos, query_seg, key_pos, key_seg)
        key_rows = lax.dynamic_slice_in_dim(key_all, first, key_block, 0).reshape(
            key_block, kv_local, HD
        )
        value_rows = lax.dynamic_slice_in_dim(value_all, first, key_block, 0).reshape(
            key_block, kv_local, HD
        )
        return (visible, key_rows, value_rows)

    def forward_step(state_now, block_index):
        visible, key_rows, value_rows = block_view(block_index)
        run_max, run_sum, run_acc = state_now
        scores = (
            jnp.einsum("tkgd,skd->kgts", q_four, key_rows, preferred_element_type=jnp.float32)
            * score_scale
        )
        masked = jnp.where(visible, scores, NEG)
        new_max = jnp.maximum(run_max, jnp.max(masked, axis=-1))
        weights = jnp.where(visible, jnp.exp(masked - new_max[..., None]), 0.0)
        factor = jnp.exp(run_max - new_max)
        run_sum = run_sum * factor + jnp.sum(weights, axis=-1)
        added = jnp.einsum(
            "kgts,skd->kgtd",
            weights.astype(jnp.bfloat16),
            value_rows,
            preferred_element_type=jnp.float32,
        )
        run_acc = run_acc * factor[..., None] + added
        state_now = (new_max, run_sum, run_acc)
        return (state_now, None)

    start_state = (
        jnp.full((kv_local, group_size, tok_rows), NEG, jnp.float32),
        jnp.zeros((kv_local, group_size, tok_rows), jnp.float32),
        jnp.zeros((kv_local, group_size, tok_rows, HD), jnp.float32),
    )
    (run_max, run_sum, run_acc), unused = lax.scan(
        forward_step, start_state, jnp.arange(block_count, dtype=jnp.int32)
    )
    log_sum = run_max + jnp.log(run_sum)
    attn = (run_acc / run_sum[..., None]).astype(jnp.bfloat16)
    attn_rows = attn.transpose(2, 0, 1, 3).reshape(tok_rows, kv_local * group_size * HD)
    grad_full = lax.all_gather(grad_y, "kv", axis=1, tiled=True)
    weight_all = lax.all_gather(w_out, "ctx", axis=1, tiled=True)
    y_terms = jnp.dot(attn_rows, weight_all, preferred_element_type=jnp.float32)
    grad_attn = lax.dot_general(
        grad_full, weight_all, (((1,), (1,)), ((), ())), preferred_element_type=jnp.float32
    )
    y_out = lax.psum_scatter(y_terms.astype(jnp.bfloat16), "kv", scatter_dimension=1, tiled=True)
    grad_four = grad_attn.astype(jnp.bfloat16).reshape(tok_rows, kv_local, group_size, HD)
    attn_four = attn_rows.reshape(tok_rows, kv_local, group_size, HD)
    delta = jnp.einsum("tkgd,tkgd->kgt", attn_four, grad_four, preferred_element_type=jnp.float32)

    def backward_step(query_grad, block_index):
        visible, key_rows, value_rows = block_view(block_index)
        grad_in = query_grad
        scores = (
            jnp.einsum("tkgd,skd->kgts", q_four, key_rows, preferred_element_type=jnp.float32)
            * score_scale
        )
        masked = jnp.where(visible, scores, NEG)
        probs = jnp.where(visible, jnp.exp(masked - log_sum[..., None]), 0.0)
        value_grad = jnp.einsum(
            "kgts,tkgd->skd",
            probs.astype(jnp.bfloat16),
            grad_four,
            preferred_element_type=jnp.float32,
        )
        prob_grad = jnp.einsum(
            "tkgd,skd->kgts", grad_four, value_rows, preferred_element_type=jnp.float32
        )
        score_grad = (probs * (prob_grad - delta[..., None])).astype(jnp.bfloat16)
        grad_in = (
            grad_in
            + jnp.einsum("kgts,skd->tkgd", score_grad, key_rows, preferred_element_type=jnp.float32)
            * score_scale
        )
        key_grad = (
            jnp.einsum("kgts,tkgd->skd", score_grad, q_four, preferred_element_type=jnp.float32)
            * score_scale
        )
        query_grad, key_grad, value_grad = (grad_in, key_grad, value_grad)
        return (query_grad, (key_grad, value_grad))

    start_grad = jnp.zeros((tok_rows, kv_local, group_size, HD), jnp.float32)
    query_grad, (key_parts, value_parts) = lax.scan(
        backward_step, start_grad, jnp.arange(block_count, dtype=jnp.int32)
    )
    key_terms = key_parts.reshape(total_rows, kv_local * HD)
    value_terms = value_parts.reshape(total_rows, kv_local * HD)
    key_sum, value_sum = (
        lax.psum_scatter(
            key_terms.astype(jnp.bfloat16), "ctx", scatter_dimension=0, tiled=True
        ).astype(jnp.float32),
        lax.psum_scatter(
            value_terms.astype(jnp.bfloat16), "ctx", scatter_dimension=0, tiled=True
        ).astype(jnp.float32),
    )
    grad_q = query_grad.reshape(tok_rows, kv_local * group_size * HD).astype(jnp.bfloat16)
    return (y_out, grad_q, key_sum.astype(jnp.bfloat16), value_sum.astype(jnp.bfloat16))


def solution(mesh):
    placed = (P("ctx", "kv"), P("ctx", "kv"), P("ctx", "kv"), P("kv", "ctx"), P("ctx", "kv"), P())
    return jax.shard_map(
        local,
        mesh=mesh,
        in_specs=placed,
        out_specs=(P("ctx", "kv"), P("ctx", "kv"), P("ctx", "kv"), P("ctx", "kv")),
        check_vma=False,
    )
```

profile of v0, /device:TPU:1, one launch (start us, length us, event | category | flops | bytes accessed | tf_op | source)
XLA Modules:
  0.0 584.9 jit_solution(1935082591754930303)
XLA Ops:
  14.2 43.8 %all-gather.5.cloned.1.call-done = bf16[3072,512]{1,0:T(8,128)(2,1)} async-done(((bf16[192,512]{1,0:T(8,128)(2,1)}), bf16[3072,512]{1,0:T(8,128)(2,1)}) %all-gather.5.cloned.1.call-update) | async-done | bytes 3145744 | tf_op jit(solution)/shard_map/all_gather | solution.py:44
  58.0 4.7 copy.56
  62.7 41.6 %all-gather.7.cloned.1.call-done = bf16[3072,512]{1,0:T(8,128)(2,1)} async-done(((bf16[192,512]{1,0:T(8,128)(2,1)}), bf16[3072,512]{1,0:T(8,128)(2,1)}) %all-gather.7.cloned.1.call-update) | async-done | bytes 3145744 | tf_op jit(solution)/shard_map/all_gather | solution.py:45
  104.3 4.7 copy.58
  109.0 116.9 %while.34 = (s32[]{:T(128)}, f32[4,5,192]{2,1,0:T(8,128)S(1)}, f32[4,5,192]{2,1,0:T(8,128)S(1)}, f32[4,5,192,128]{3,2,1,0:T(8,128)}, s32[6]{0:T(128)S(1)}, /*ind...) while((s32[]{:T(128)}, f32[4,5,192]{2,1,0:T(8,128)S(1)}, ...), condition=%wide.region_6.7_spmd.clone, body=%wide.region_2.6_spmd.clone.sunk | while | flops 1034086848 | bytes 65867364 | solution.py:88
  117.4 5.0 fusion.87
  135.6 4.8 fusion.87
  141.6 5.5 fusion.89
  155.3 4.9 fusion.87
  161.3 5.5 fusion.89
  174.8 5.0 fusion.87
  180.9 5.6 fusion.89
  194.7 4.9 fusion.87
  200.7 5.5 fusion.89
  214.2 5.0 fusion.87
  220.4 5.6 fusion.89
  238.4 15.1 %convolution_convert_fusion = bf16[192,5120]{1,0:T(8,128)(2,1)} fusion(bf16[192,2560]{0,1:T(8,128)(2,1)} %bitcast.202, bf16[2560,5120]{0,1:T(8,128)(2,1)} %all-gather.9.cloned.1.call-done), kind=kOutput, calls=%fused_computation.60 | convolution fusion | flops 5034147840 | bytes 29163520 | tf_op jit(solution)/shard_map/dot_general | solution.py:96
  253.7 17.2 %all-gather.11.cloned.1.call-done = bf16[192,5120]{1,0:T(8,128)(2,1)} async-done(((bf16[192,2560]{1,0:T(8,128)(2,1)}), bf16[192,5120]{1,0:T(8,128)(2,1)}) %all-gather.11.cloned.1.call-update) | async-done | bytes 1966096 | tf_op jit(solution)/shard_map/all_gather | solution.py:94
  271.0 12.5 %convolution_convert_fusion.1 = bf16[192,2560]{1,0:T(8,128)(2,1)} fusion(bf16[192,5120]{1,0:T(8,128)(2,1)} %all-gather.11.cloned.1.call-done, bf16[2560,5120]{0,1:T(8,128)(2,1)} %all-gather.9.cloned.1.call-done), kind=kOutput, calls=%fused_computation.61 | convolution fusion | flops 5033656320 | bytes 29163520 | tf_op jit(solution)/shard_map/dot_general | solution.py:97
  290.7 145.6 %while.35 = (s32[]{:T(128)}, f32[192,4,5,128]{3,0,2,1:T(8,128)S(1)}, bf16[6,512,4,128]{3,1,2,0:T(8,128)(2,1)}, bf16[6,512,4,128]{3,1,2,0:T(8,128)(2,1)}, s32[6]{...) while((s32[]{:T(128)}, ...), condition=%wide.region_10.11_spmd.clone, body=%wide.region_8.10_spmd.clone.sunk | while | flops 2542313216 | bytes 161842016 | solution.py:137
  297.6 4.5 fusion.101
  322.0 4.5 fusion.101
  451.5 56.4 %reduce-scatter.6.cloned.1.call-done = bf16[192,512]{1,0:T(8,128)(2,1)} async-done(((bf16[3072,512]{1,0:T(8,128)(2,1)}), bf16[192,512]{1,0:T(8,128)(2,1)}) %reduce-scatter.6.cloned.1.call-update) | async-done | bytes 196624 | tf_op jit(solution)/shard_map/reduce_scatter | solution.py:143
  507.9 70.1 %reduce-scatter.8.cloned.1.call-done = bf16[192,512]{1,0:T(8,128)(2,1)} async-done(((bf16[3072,512]{1,0:T(8,128)(2,1)}), bf16[192,512]{1,0:T(8,128)(2,1)}) %reduce-scatter.8.cloned.1.call-update) | async-done | bytes 196624 | tf_op jit(solution)/shard_map/reduce_scatter | solution.py:146
  (341 shorter events, 229.5 us)
Async XLA Ops:
  7.2 50.8 %all-gather.5.cloned.1.call-start = ((), (), s32[]{:S(2)}) async-start(), calls=%async_computation.3 | async-start | bytes 3342336 | tf_op jit(solution)/shard_map/all_gather | solution.py:44
  7.9 96.4 %all-gather.7.cloned.1.call-start = ((), (), s32[]{:S(2)}) async-start(), calls=%async_computation.4 | async-start | bytes 3342336 | tf_op jit(solution)/shard_map/all_gather | solution.py:45
  8.7 229.7 %all-gather.9.cloned.1.call-start = ((), (), s32[]{:S(2)}) async-start(), calls=%async_computation.5 | async-start | bytes 27852800 | tf_op jit(solution)/shard_map/all_gather | solution.py:95
  9.4 261.6 %all-gather.11.cloned.1.call-start = ((), (), s32[]{:S(2)}) async-start(), calls=%async_computation.7 | async-start | bytes 2949120 | tf_op jit(solution)/shard_map/all_gather | solution.py:94
  10.0 441.5 %reduce-scatter.4.cloned.1.call-start = ((), (), s32[]{:S(2)}) async-start(), calls=%async_computation.6 | async-start | bytes 2949120 | tf_op jit(solution)/shard_map/reduce_scatter | solution.py:100
  117.4 5.0 copy-start.4
  117.4 6.1 %copy-start = (f32[4,512,192,5]{1,2,3,0:T(8,128)S(1)}, f32[4,512,192,5]{1,2,3,0:T(8,128)}, u32[]{:S(2)}) copy-start(f32[4,512,192,5]{1,2,3,0:T(8,128)} %get-tuple-element.744) | copy-start | bytes 23592964 | tf_op jit(solution)/shard_map/while
  135.6 6.1 %copy-start = (f32[4,512,192,5]{1,2,3,0:T(8,128)S(1)}, f32[4,512,192,5]{1,2,3,0:T(8,128)}, u32[]{:S(2)}) copy-start(f32[4,512,192,5]{1,2,3,0:T(8,128)} %get-tuple-element.744) | copy-start | bytes 23592964 | tf_op jit(solution)/shard_map/while
  155.3 4.9 copy-start.4
  155.3 6.0 %copy-start = (f32[4,512,192,5]{1,2,3,0:T(8,128)S(1)}, f32[4,512,192,5]{1,2,3,0:T(8,128)}, u32[]{:S(2)}) copy-start(f32[4,512,192,5]{1,2,3,0:T(8,128)} %get-tuple-element.744) | copy-start | bytes 23592964 | tf_op jit(solution)/shard_map/while
  174.8 5.0 copy-start.4
  174.8 6.1 %copy-start = (f32[4,512,192,5]{1,2,3,0:T(8,128)S(1)}, f32[4,512,192,5]{1,2,3,0:T(8,128)}, u32[]{:S(2)}) copy-start(f32[4,512,192,5]{1,2,3,0:T(8,128)} %get-tuple-element.744) | copy-start | bytes 23592964 | tf_op jit(solution)/shard_map/while
  194.7 4.9 copy-start.4
  194.7 6.0 %copy-start = (f32[4,512,192,5]{1,2,3,0:T(8,128)S(1)}, f32[4,512,192,5]{1,2,3,0:T(8,128)}, u32[]{:S(2)}) copy-start(f32[4,512,192,5]{1,2,3,0:T(8,128)} %get-tuple-element.744) | copy-start | bytes 23592964 | tf_op jit(solution)/shard_map/while
  214.2 5.1 copy-start.4
  214.2 6.2 %copy-start = (f32[4,512,192,5]{1,2,3,0:T(8,128)S(1)}, f32[4,512,192,5]{1,2,3,0:T(8,128)}, u32[]{:S(2)}) copy-start(f32[4,512,192,5]{1,2,3,0:T(8,128)} %get-tuple-element.744) | copy-start | bytes 23592964 | tf_op jit(solution)/shard_map/while
  253.5 254.4 %reduce-scatter.6.cloned.1.call-start = ((), (), s32[]{:S(2)}) async-start(), calls=%async_computation.8 | async-start | bytes 3342336 | tf_op jit(solution)/shard_map/reduce_scatter | solution.py:143
  308.2 6.8 %copy-start.6 = (bf16[6,512,4,128]{3,1,2,0:T(8,128)(2,1)}, bf16[6,512,4,128]{3,1,2,0:T(8,128)(2,1)S(1)}, u32[]{:S(2)}) copy-start(bf16[6,512,4,128]{3,1,2,0:T(8,128)(2,1)S(1)} %fusion.102) | copy-start | bytes 9437188 | tf_op jit(solution)/shard_map/while
  332.5 6.8 %copy-start.6 = (bf16[6,512,4,128]{3,1,2,0:T(8,128)(2,1)}, bf16[6,512,4,128]{3,1,2,0:T(8,128)(2,1)S(1)}, u32[]{:S(2)}) copy-start(bf16[6,512,4,128]{3,1,2,0:T(8,128)(2,1)S(1)} %fusion.102) | copy-start | bytes 9437188 | tf_op jit(solution)/shard_map/while
  356.7 6.8 %copy-start.6 = (bf16[6,512,4,128]{3,1,2,0:T(8,128)(2,1)}, bf16[6,512,4,128]{3,1,2,0:T(8,128)(2,1)S(1)}, u32[]{:S(2)}) copy-start(bf16[6,512,4,128]{3,1,2,0:T(8,128)(2,1)S(1)} %fusion.102) | copy-start | bytes 9437188 | tf_op jit(solution)/shard_map/while
  381.0 6.8 %copy-start.6 = (bf16[6,512,4,128]{3,1,2,0:T(8,128)(2,1)}, bf16[6,512,4,128]{3,1,2,0:T(8,128)(2,1)S(1)}, u32[]{:S(2)}) copy-start(bf16[6,512,4,128]{3,1,2,0:T(8,128)(2,1)S(1)} %fusion.102) | copy-start | bytes 9437188 | tf_op jit(solution)/shard_map/while
  405.2 6.8 %copy-start.6 = (bf16[6,512,4,128]{3,1,2,0:T(8,128)(2,1)}, bf16[6,512,4,128]{3,1,2,0:T(8,128)(2,1)S(1)}, u32[]{:S(2)}) copy-start(bf16[6,512,4,128]{3,1,2,0:T(8,128)(2,1)S(1)} %fusion.102) | copy-start | bytes 9437188 | tf_op jit(solution)/shard_map/while
  429.5 6.8 %copy-start.6 = (bf16[6,512,4,128]{3,1,2,0:T(8,128)(2,1)}, bf16[6,512,4,128]{3,1,2,0:T(8,128)(2,1)S(1)}, u32[]{:S(2)}) copy-start(bf16[6,512,4,128]{3,1,2,0:T(8,128)(2,1)S(1)} %fusion.102) | copy-start | bytes 9437188 | tf_op jit(solution)/shard_map/while
  442.8 135.3 %reduce-scatter.8.cloned.1.call-start = ((), (), s32[]{:S(2)}) async-start(), calls=%async_computation.9 | async-start | bytes 3342336 | tf_op jit(solution)/shard_map/reduce_scatter | solution.py:146
  (50 other events, 199.6 us)
Sparse Core Ops, SparseCore 0:
  10.3 47.6 all-gather.4
  60.3 43.9 all-gather.6
  105.9 132.3 all-gather.8
  239.8 31.1 all-gather.10
  273.6 30.3 reduce-scatter.3
  442.9 64.9 reduce-scatter.5
  512.8 65.2 reduce-scatter.7
where the time goes:
time: 588 us; the launch traced here: 585 us
  waiting for transfers between devices  236 us (40%)
  matrix products  178 us (30%)
  local copies, waits for them, and re-layouts  108 us (18%)
  other arithmetic  39.8 us (7%)
  between operations  14.2 us (2%)
  loops' own time  8.93 us (2%)
    reduce_scatter x1, waiting for transfers between devices, local(): lax.psum_scatter(value_terms.astype(jnp.bfloat16), 'ctx', scatter_dimensi...  70.1 us
    reduce_scatter x1, waiting for transfers between devices, local(): lax.psum_scatter(key_terms.astype(jnp.bfloat16), 'ctx', scatter_dimension...  56.4 us
    all_gather x1, waiting for transfers between devices, local(): lax.all_gather(keys, 'ctx', axis=0, tiled=True)  43.8 us
    while x138, local copies, waits for them, and re-layouts  42.8 us
    all_gather x1, waiting for transfers between devices, local(): lax.all_gather(values, 'ctx', axis=0, tiled=True)  41.6 us
    dot_general x6, matrix products, forward_step(): jnp.einsum('kgts,skd->kgtd', weights.astype(jnp.bfloat16), value_rows, pr...  31.6 us
    reduce_sum x6, other arithmetic, forward_step(): run_sum = run_sum * factor + jnp.sum(weights, axis=-1)  29.5 us
    dot_general x6, matrix products, backward_step(): jnp.einsum('tkgd,skd->kgts', grad_four, value_rows, preferred_element_typ...  26.7 us
  transfers between devices with their start and end apart: 7, of which 6 were waited for; matrix products, arithmetic and copies ran while one was open for 48% of the time, Pallas kernels for 0%

commit v1 on v0

v1 whole, which is shorter than its diff:
```python
import functools
import math

import jax
import jax.numpy as jnp
from jax import lax
from jax.experimental import pallas as pl
from jax.experimental.pallas import tpu as pltpu
from jax.sharding import Mesh, PartitionSpec as P

H = 40
KVH = 8
HD = 128
BLK = 128
NRESP = 4
G = H // KVH
KB = 256
NEG = -1e30
SCALE = 1.0 / math.sqrt(HD)
C2 = SCALE * math.log2(math.e)
NT = (((1,), (1,)), ((), ()))
NN = (((1,), (0,)), ((), ()))


def dot(a, b, dims=NN):
    return lax.dot_general(a, b, dims, preferred_element_type=jnp.float32)


def seg_start(info, pos, prompt):
    start = jnp.where(pos >= info[1], info[1], prompt)
    start = jnp.where(pos >= info[2], info[2], start)
    return jnp.where(pos >= info[3], info[3], start)


def block_range(info, q_first, q_rows, prompt):
    full = jnp.minimum(prompt, q_first + 1) // KB
    first = jnp.where(q_first >= prompt, seg_start(info, q_first, prompt) // KB, full)
    last = (q_first + q_rows - 1) // KB + 1
    return full, first, last


def visible(info, q_first, q_rows, k_first, prompt):
    q_pos = q_first + lax.broadcasted_iota(jnp.int32, (1, q_rows), 1)
    start = seg_start(info, q_pos, prompt)
    k_pos = k_first + lax.broadcasted_iota(jnp.int32, (KB, q_rows), 0)
    return (k_pos <= q_pos) & ((k_pos < prompt) | (k_pos >= start))


def read_info(info_ref):
    return [info_ref[i] for i in range(4)]


def fwd_kernel(prompt, qb, info_ref, q_ref, k_ref, vt_ref, o_ref, lse_ref, m_ref, l_ref, acc_ref):
    info = read_info(info_ref)
    blocks = q_ref.shape[0] // qb

    def query_block(i, carry):
        rows = pl.ds(pl.multiple_of(i * qb, qb), qb)
        q_first = info[0] + i * qb
        m_ref[...] = jnp.full_like(m_ref, NEG)
        l_ref[...] = jnp.zeros_like(l_ref)
        acc_ref[...] = jnp.zeros_like(acc_ref)
        full, first, last = block_range(info, q_first, qb, prompt)

        def key_block(masked, b, carry):
            keys = pl.ds(pl.multiple_of(b * KB, KB), KB)
            k_blk = k_ref[keys, :]
            vt_blk = vt_ref[:, keys]
            vis = visible(info, q_first, qb, b * KB, prompt) if masked else None
            for h in range(G):
                s = dot(k_blk, q_ref[rows, h * HD:(h + 1) * HD], NT) * C2
                if masked:
                    s = jnp.where(vis, s, NEG)
                m_old = m_ref[h:h + 1, :]
                m_new = jnp.maximum(m_old, jnp.max(s, axis=0, keepdims=True))
                p = jnp.exp2(s - m_new)
                alpha = jnp.exp2(m_old - m_new)
                m_ref[h:h + 1, :] = m_new
                l_ref[h:h + 1, :] = l_ref[h:h + 1, :] * alpha + jnp.sum(p, axis=0, keepdims=True)
                acc_ref[h] = acc_ref[h] * alpha + dot(vt_blk, p.astype(jnp.bfloat16))
            return carry

        lax.fori_loop(0, full, functools.partial(key_block, False), 0)
        lax.fori_loop(first, last, functools.partial(key_block, True), 0)
        for h in range(G):
            l = l_ref[h:h + 1, :]
            o_ref[rows, h * HD:(h + 1) * HD] = (acc_ref[h] / l).T.astype(jnp.bfloat16)
            lse_ref[i, h:h + 1, :] = m_ref[h:h + 1, :] + jnp.log2(l)
        return carry

    lax.fori_loop(0, blocks, query_block, 0)


def bwd_kernel(prompt, qb, info_ref, q_ref, k_ref, kt_ref, v_ref, o_ref, lse_ref, do_ref,
               dq_ref, dkv_ref, qs_ref, dos_ref, del_ref, p_ref, ds_ref, dqt_ref, dk_ref, dv_ref):
    info = read_info(info_ref)
    blocks = q_ref.shape[0] // qb
    dk_ref[...] = jnp.zeros_like(dk_ref)
    dv_ref[...] = jnp.zeros_like(dv_ref)

    def query_block(i, carry):
        rows = pl.ds(pl.multiple_of(i * qb, qb), qb)
        q_first = info[0] + i * qb
        for h in range(G):
            cols = slice(h * HD, (h + 1) * HD)
            do = do_ref[rows, cols]
            qs_ref[h * qb:(h + 1) * qb, :] = q_ref[rows, cols]
            dos_ref[h * qb:(h + 1) * qb, :] = do
            prod = do.astype(jnp.float32) * o_ref[rows, cols].astype(jnp.float32)
            del_ref[h:h + 1, :] = jnp.sum(prod.T, axis=0, keepdims=True)
        dqt_ref[...] = jnp.zeros_like(dqt_ref)
        full, first, last = block_range(info, q_first, qb, prompt)

        def key_block(masked, b, carry):
            keys = pl.ds(pl.multiple_of(b * KB, KB), KB)
            k_blk = k_ref[keys, :]
            v_blk = v_ref[keys, :]
            vis = visible(info, q_first, qb, b * KB, prompt) if masked else None
            for h in range(G):
                part = slice(h * qb, (h + 1) * qb)
                s = dot(k_blk, qs_ref[part, :], NT) * C2
                p = jnp.exp2(s - lse_ref[i, h:h + 1, :])
                if masked:
                    p = jnp.where(vis, p, 0.0)
                dp = dot(v_blk, dos_ref[part, :], NT)
                p_ref[h] = p.astype(jnp.bfloat16)
                ds_ref[h] = (p * (dp - del_ref[h:h + 1, :])).astype(jnp.bfloat16)
            dv = jnp.zeros((KB, HD), jnp.float32)
            dk = jnp.zeros((KB, HD), jnp.float32)
            for h in range(G):
                part = slice(h * qb, (h + 1) * qb)
                dv += dot(p_ref[h], dos_ref[part, :])
                dk += dot(ds_ref[h], qs_ref[part, :])
                dqt_ref[h] += dot(kt_ref[:, keys], ds_ref[h])
            dv_ref[keys, :] += dv
            dk_ref[keys, :] += dk
            return carry

        lax.fori_loop(0, full, functools.partial(key_block, False), 0)
        lax.fori_loop(first, last, functools.partial(key_block, True), 0)
        for h in range(G):
            dq_ref[rows, h * HD:(h + 1) * HD] = (dqt_ref[h] * SCALE).T.astype(jnp.bfloat16)
        return carry

    lax.fori_loop(0, blocks, query_block, 0)
    dkv_ref[:, :HD] = (dk_ref[...] * SCALE).astype(jnp.bfloat16)
    dkv_ref[:, HD:] = dv_ref[...].astype(jnp.bfloat16)


VM = pl.BlockSpec(memory_space=pltpu.VMEM)
SM = pl.BlockSpec(memory_space=pltpu.SMEM)


def fwd_attention(info, q, k, vt, prompt, qb):
    rows, keys = q.shape[0], k.shape[0]
    work = G * rows * keys
    return pl.pallas_call(
        functools.partial(fwd_kernel, prompt, qb),
        out_shape=(
            jax.ShapeDtypeStruct((rows, G * HD), jnp.bfloat16),
            jax.ShapeDtypeStruct((rows // qb, 8, qb), jnp.float32),
        ),
        in_specs=[SM, VM, VM, VM],
        out_specs=(VM, VM),
        scratch_shapes=[
            pltpu.VMEM((8, qb), jnp.float32),
            pltpu.VMEM((8, qb), jnp.float32),
            pltpu.VMEM((G, HD, qb), jnp.float32),
        ],
        compiler_params=pltpu.CompilerParams(vmem_limit_bytes=24 << 20),
        cost_estimate=pl.CostEstimate(flops=work * HD * 4 * 2, bytes_accessed=4 << 20, transcendentals=work),
        name="attention_fwd",
    )(info, q, k, vt)


def bwd_attention(info, q, k, kt, v, o, lse, do, prompt, qb):
    rows, keys = q.shape[0], k.shape[0]
    work = G * rows * keys
    return pl.pallas_call(
        functools.partial(bwd_kernel, prompt, qb),
        out_shape=(
            jax.ShapeDtypeStruct((rows, G * HD), jnp.bfloat16),
            jax.ShapeDtypeStruct((keys, 2 * HD), jnp.bfloat16),
        ),
        in_specs=[SM] + [VM] * 7,
        out_specs=(VM, VM),
        scratch_shapes=[
            pltpu.VMEM((G * qb, HD), jnp.bfloat16),
            pltpu.VMEM((G * qb, HD), jnp.bfloat16),
            pltpu.VMEM((8, qb), jnp.float32),
            pltpu.VMEM((G, KB, qb), jnp.bfloat16),
            pltpu.VMEM((G, KB, qb), jnp.bfloat16),
            pltpu.VMEM((G, HD, qb), jnp.float32),
            pltpu.VMEM((keys, HD), jnp.float32),
            pltpu.VMEM((keys, HD), jnp.float32),
        ],
        compiler_params=pltpu.CompilerParams(vmem_limit_bytes=32 << 20),
        cost_estimate=pl.CostEstimate(flops=work * HD * 10 * 2, bytes_accessed=8 << 20, transcendentals=work),
        name="attention_bwd",
    )(info, q, k, kt, v, o, lse, do)


def local(queries, keys, values, w_out, grad_y, resp_blocks):
    heads = lax.axis_size("hd")
    tok = queries.shape[0]
    rows = tok * heads
    total = rows * lax.axis_size("tg")
    prompt = total // 2
    qb = 256 if rows % 256 == 0 else rows
    first = lax.axis_index("tg").astype(jnp.int32) * rows
    ends = prompt + jnp.cumsum(resp_blocks[: NRESP - 1]).astype(jnp.int32) * BLK
    info = jnp.concatenate([first[None], ends])

    def a2a(x, split, concat):
        return lax.all_to_all(x, "hd", split, concat, tiled=True) if heads > 1 else x

    kv = jnp.concatenate([keys.reshape(tok, heads, HD), values.reshape(tok, heads, HD)], axis=2)
    kv = a2a(kv.reshape(tok, heads * 2 * HD), 1, 0)
    kv = lax.all_gather(kv, "tg", axis=0, tiled=True)
    q = a2a(queries, 1, 0)
    wt = a2a(w_out.T, 1, 0)
    wt = lax.all_gather(wt, "tg", axis=0, tiled=True)
    gy = lax.all_gather(grad_y, "kv", axis=1, tiled=True)
    gy = lax.all_gather(gy, "hd", axis=0, tiled=True)
    k, v = kv[:, :HD], kv[:, HD:]
    attn, lse = fwd_attention(info, q, k, v.T, prompt, qb)
    grad_attn = jnp.dot(gy, wt, preferred_element_type=jnp.float32).astype(jnp.bfloat16)
    y = dot(attn, wt, NT).astype(jnp.bfloat16)
    y = lax.psum_scatter(y, "hd", scatter_dimension=0, tiled=True)
    y = lax.psum_scatter(y, "kv", scatter_dimension=1, tiled=True)
    dq, dkv = bwd_attention(info, q, k, k.T, v, attn, lse, grad_attn, prompt, qb)
    dkv = lax.psum_scatter(dkv, "tg", scatter_dimension=0, tiled=True)
    dkv = a2a(dkv, 0, 1).reshape(tok, heads, 2, HD)
    dq = a2a(dq, 0, 1)
    return (y, dq, dkv[:, :, 0].reshape(tok, heads * HD), dkv[:, :, 1].reshape(tok, heads * HD))


def solution(mesh):
    ctx, n_kv = mesh.devices.shape
    heads = KVH // n_kv
    split = Mesh(mesh.devices.reshape(ctx // heads, heads, n_kv), ("tg", "hd", "kv"))
    tok = ("tg", "hd")
    tiled = P(tok, "kv")
    return jax.shard_map(
        local,
        mesh=split,
        in_specs=(tiled, tiled, tiled, P("kv", tok), tiled, P()),
        out_specs=(tiled,) * 4,
        check_vma=False,
    )
```

time: 588 us -> 407 us (0.69)
  matrix products: 178 us -> 21.5 us
  local copies, waits for them, and re-layouts: 108 us -> 15.8 us
  blocking collectives: 0 us -> 51.3 us
  other arithmetic: 39.8 us -> 0.31 us
  waiting for transfers between devices: 236 us -> 273 us
  Pallas kernels: 0 us -> 19.8 us
  loops' own time: 8.93 us -> 0 us
  starting transfers between devices: 0.45 us -> 8.91 us
    dot_general x44 -> x2, matrix products: 178 us -> 21.5 us  [the longest x1 10.9 us: dot(): return lax.dot_general(a, b, dims, preferred_element_type=jnp.float32)]
    all_gather x4, waiting for transfers between devices: 107 us -> 176 us  [the longest x1 104 us: local(): wt = lax.all_gather(wt, 'tg', axis=0, tiled=True)]
    all_to_all x0 -> x3, blocking collectives: none -> 51.3 us  [a2a(): lax.all_to_all(x, 'hd', split, concat, tiled=True)]
    while x138 -> x0, local copies, waits for them, and re-layouts: 42.8 us -> none
    reduce_scatter x3, waiting for transfers between devices: 127 us -> 90.8 us  [the longest x1 50.8 us: local(): y = lax.psum_scatter(y, 'hd', scatter_dimension=0, tiled=True)]
    reduce_sum x19 -> x0, other arithmetic: 30.6 us -> none  [the longest x6 29.5 us: forward_step(): run_sum = run_sum * factor + jnp.sum(weights, axis=-1)]
    dynamic_slice x24 -> x0, local copies, waits for them, and re-layouts: 27.7 us -> none  [the longest x12 20.7 us: block_view(): lax.dynamic_slice_in_dim(value_all, first, key_block, 0)]
    pallas_call x0 -> x2, Pallas kernels: none -> 19.8 us  [the longest x1 10.4 us: fwd_attention(): pl.pallas_call(functools.partial(fwd_kernel, prompt, qb), out_shape=(jax....]
  transfers between devices with their start and end apart: 7 -> 9, of which waited for: 6 -> 7; matrix products, arithmetic and copies ran while one was open for 48% -> 8% of each run, Pallas kernels for 0% -> 5%
where the time goes in v1:
time: 407 us; the launch traced here: 405 us
  waiting for transfers between devices  273 us (67%)
  blocking collectives  51.3 us (13%)
  matrix products  21.5 us (5%)
  Pallas kernels  19.8 us (5%)
  local copies, waits for them, and re-layouts  15.8 us (4%)
  between operations  14.3 us (4%)
  starting transfers between devices  8.91 us (2%)
    all_gather x1, waiting for transfers between devices, local(): wt = lax.all_gather(wt, 'tg', axis=0, tiled=True)  104 us
    all_to_all x3, blocking collectives, a2a(): lax.all_to_all(x, 'hd', split, concat, tiled=True)  51.3 us
    reduce_scatter x1, waiting for transfers between devices, local(): y = lax.psum_scatter(y, 'hd', scatter_dimension=0, tiled=True)  50.8 us
    all_gather x1, waiting for transfers between devices, local(): gy = lax.all_gather(gy, 'hd', axis=0, tiled=True)  41.8 us
    all_gather x1, waiting for transfers between devices, local(): kv = lax.all_gather(kv, 'tg', axis=0, tiled=True)  29.8 us
    reduce_scatter x1, waiting for transfers between devices, local(): dkv = lax.psum_scatter(dkv, 'tg', scatter_dimension=0, tiled=True)  21 us
    reduce_scatter x1, waiting for transfers between devices, local(): y = lax.psum_scatter(y, 'kv', scatter_dimension=1, tiled=True)  18.9 us
    dot_general x1, matrix products, dot(): return lax.dot_general(a, b, dims, preferred_element_type=jnp.float32)  10.9 us
  transfers between devices with their start and end apart: 9, of which 7 were waited for; matrix products, arithmetic and copies ran while one was open for 8% of the time, Pallas kernels for 5%

profile of v1, /device:TPU:1, one launch (start us, length us, event | category | flops | bytes accessed | tf_op | source)
XLA Modules:
  0.0 405.3 jit_solution(4741510636888546805)
XLA Ops:
  8.1 1.1 copy_bitcast_fusion.4
  9.3 10.6 %all_to_all.89 = bf16[192,4,256]{2,0,1:T(8,128)(2,1)} all-to-all(bf16[192,4,256]{2,0,1:T(8,128)(2,1)S(1)} %pad_maximum_fusion), channel_id=1, replica_groups=mesh['tg'=4,'hd'=4,'kv'=2] {'hd'}, dimensions={1} | all-to-all | bytes 786432 | tf_op jit(solution)/shard_map/all_to_all | solution.py:215
  19.9 1.7 copy.59
  21.6 24.4 %all_to_all.90 = bf16[320,4,640]{2,0,1:T(8,128)(2,1)} all-to-all(bf16[320,4,640]{2,0,1:T(8,128)(2,1)S(1)} %bitcast.65), channel_id=1, replica_groups=mesh['tg'=4,'hd'=4,'kv'=2] {'hd'}, dimensions={1} | all-to-all | bytes 3276800 | tf_op jit(solution)/shard_map/all_to_all | solution.py:215
  47.6 4.2 %all-to-all-start = ((bf16[192,4,640]{2,0,1:T(8,128)(2,1)}), bf16[192,4,640]{2,0,1:T(8,128)(2,1)S(1)}, u32[]{:S(2)}, u32[]{:S(2)}) async-start(bf16[192,4,640]{2,0,1:T(8,128)(2,1)} %bitcast.58), calls=%async_computation | async-start | bytes 1966080 | tf_op jit(solution)/shard_map/all_to_all | solution.py:215
  52.1 29.8 %all-gather.5.cloned.1.call-done = bf16[3072,256]{1,0:T(8,128)(2,1)} async-done(((bf16[768,256]{1,0:T(8,128)(2,1)}), bf16[3072,256]{1,0:T(8,128)(2,1)}) %all-gather.5.cloned.1.call-update) | async-done | bytes 1572880 | tf_op jit(solution)/shard_map/all_gather | solution.py:219
  81.9 2.7 fusion
  84.6 1.3 copy.38.vt_ref
  85.8 1.1 copy-done.4
  86.9 10.4 %attention_fwd.1 = (bf16[768,640]{1,0:T(8,128)(2,1)S(1)}, f32[3,8,256]{2,1,0:T(8,128)S(1)}) custom-call(s32[4]{0:T(128)S(1)} %pad_add_fusion.info_ref, bf16[768,640]{1,0:T(8,128)(2,1)S(1)} %bitcast.61, bf16[3072,128]{1,0:T(8,128)(2,1)S(1)} %get-tuple-element.15.k_ref, bf16[128,3072]{1,0:T(8,128)(2,1)S(1)} %copy-done.4), custom_call_target="tpu_custom_call" | custom-call | flops 12079595520 | bytes 4194304 | tf_op jit(solution)/shard_map/attention_fwd/pallas_call | solution.py:157
  98.3 104.0 %all-gather.7.cloned.1.call-done = bf16[5120,640]{1,0:T(8,128)(2,1)} async-done(((bf16[1280,640]{1,0:T(8,128)(2,1)}), bf16[5120,640]{1,0:T(8,128)(2,1)}) %all-gather.7.cloned.1.call-update) | async-done | bytes 6553616 | tf_op jit(solution)/shard_map/all_gather | solution.py:222
  202.4 10.9 %convolution_convert_fusion = bf16[768,5120]{1,0:T(8,128)(2,1)} fusion(bf16[768,640]{1,0:T(8,128)(2,1)} %copy-done.5, bf16[5120,640]{1,0:T(8,128)(2,1)} %all-gather.7.cloned.1.call-done), kind=kOutput, calls=%fused_computation | convolution fusion | flops 5037096960 | bytes 15400960 | tf_op jit(solution)/shard_map/dot_general | solution.py:26
  213.5 1.1 copy-done.7
  214.6 1.2 copy.40.kt_ref
  215.8 41.8 %all-gather.11.cloned.1.call-done = bf16[768,5120]{1,0:T(8,128)(2,1)} async-done(((bf16[192,5120]{1,0:T(8,128)(2,1)}), bf16[768,5120]{1,0:T(8,128)(2,1)}) %all-gather.11.cloned.1.call-update) | async-done | bytes 7864336 | tf_op jit(solution)/shard_map/all_gather | solution.py:224
  257.6 10.6 %convolution_convert_fusion.1.do_ref = bf16[768,640]{1,0:T(8,128)(2,1)S(1)} fusion(bf16[768,5120]{1,0:T(8,128)(2,1)} %all-gather.11.cloned.1.call-done, bf16[5120,640]{1,0:T(8,128)(2,1)} %all-gather.7.cloned.1.call-done), kind=kOutput, calls=%fused_computation.2 | convolution fusion | flops 5033656320 | bytes 15400960 | tf_op jit(solution)/shard_map/dot_general | solution.py:227
  268.3 9.4 %attention_bwd.1 = (bf16[768,640]{1,0:T(8,128)(2,1)S(1)}, bf16[3072,256]{1,0:T(8,128)(2,1)}) custom-call(s32[4]{0:T(128)S(1)} %pad_add_fusion.info_ref, bf16[768,640]{1,0:T(8,128)(2,1)S(1)} %bitcast.62, bf16[3072,128]{1,0:T(8,128)(2,1)S(1)} %copy-done.2, bf16[128,3072]{1,0:T(8,128)(2,1)S(1)} %copy-done.3, bf16[3072,128]{1,0:T(8,128)(2,1)S(1)} %get-tuple-element.12.v_ref, ...), custom_call_target="tpu_custom_call" | custom-call | flops 30198988800 | bytes 8388608 | tf_op jit(solution)/shard_map/attention_bwd/pallas_call | solution.py:179
  277.7 50.8 %reduce-scatter.4.cloned.1.call-done = bf16[192,5120]{1,0:T(8,128)(2,1)} async-done(((bf16[768,5120]{1,0:T(8,128)(2,1)}), bf16[192,5120]{1,0:T(8,128)(2,1)}) %reduce-scatter.4.cloned.1.call-update) | async-done | bytes 1966096 | tf_op jit(solution)/shard_map/reduce_scatter | solution.py:229
  328.6 16.4 %all_to_all.91 = bf16[4,192,640]{2,1,0:T(8,128)(2,1)S(1)} all-to-all(bf16[4,192,640]{2,1,0:T(8,128)(2,1)S(1)} %bitcast.63), channel_id=1, replica_groups=mesh['tg'=4,'hd'=4,'kv'=2] {'hd'}, dimensions={0} | all-to-all | bytes 1966080 | tf_op jit(solution)/shard_map/all_to_all | solution.py:215
  345.0 21.0 %reduce-scatter.8.cloned.1.call-done = bf16[768,256]{1,0:T(8,128)(2,1)} async-done(((bf16[3072,256]{1,0:T(8,128)(2,1)}), bf16[768,256]{1,0:T(8,128)(2,1)}) %reduce-scatter.8.cloned.1.call-update) | async-done | bytes 393232 | tf_op jit(solution)/shard_map/reduce_scatter | solution.py:232
  366.0 4.3 %all-to-all-start.4 = ((bf16[4,192,256]{2,1,0:T(8,128)(2,1)}), bf16[4,192,256]{2,1,0:T(8,128)(2,1)S(1)}, u32[]{:S(2)}, u32[]{:S(2)}) async-start(bf16[4,192,256]{2,1,0:T(8,128)(2,1)} %bitcast.74), calls=%async_computation.7 | async-start | bytes 786432 | tf_op jit(solution)/shard_map/all_to_all | solution.py:215
  370.3 1.0 copy.50
  371.3 5.6 %all-to-all-done.4 = bf16[4,192,256]{2,1,0:T(8,128)(2,1)S(1)} async-done(((bf16[4,192,256]{2,1,0:T(8,128)(2,1)}), bf16[4,192,256]{2,1,0:T(8,128)(2,1)S(1)}, u32[]{:S(2)}, u32[]{:S(2)}) %all-to-all-start.4) | async-done | bytes 393248 | tf_op jit(solution)/shard_map/all_to_all | solution.py:215
  379.5 18.9 %reduce-scatter.6.cloned.1.call-done = bf16[192,2560]{1,0:T(8,128)(2,1)} async-done(((bf16[192,5120]{1,0:T(8,128)(2,1)}), bf16[192,2560]{1,0:T(8,128)(2,1)}) %reduce-scatter.6.cloned.1.call-update) | async-done | bytes 983056 | tf_op jit(solution)/shard_map/reduce_scatter | solution.py:230
  (46 shorter events, 6.7 us)
Async XLA Ops:
  7.2 0.9 copy-start
  7.2 38.9 %all-gather.9.cloned.1.call-start = ((), (), s32[]{:S(2)}) async-start(), calls=%async_computation.12 | async-start | bytes 2949120 | tf_op jit(solution)/shard_map/all_gather | solution.py:223
  7.9 38.6 %copy-start.8 = (bf16[192,2560]{1,0:T(8,128)(2,1)S(1)}, bf16[192,2560]{1,0:T(8,128)(2,1)}, u32[]{:S(2)}) copy-start(bf16[192,2560]{1,0:T(8,128)(2,1)} %param.6) | copy-start | bytes 2949124
  7.9 74.0 %all-gather.5.cloned.1.call-start = ((), (), s32[]{:S(2)}) async-start(), calls=%async_computation.8 | async-start | bytes 1966080 | tf_op jit(solution)/shard_map/all_gather | solution.py:219
  19.8 182.5 %all-gather.7.cloned.1.call-start = ((), (), s32[]{:S(2)}) async-start(), calls=%async_computation.9 | async-start | bytes 8192000 | tf_op jit(solution)/shard_map/all_gather | solution.py:222
  19.9 31.9 %copy-start.9 = (s32[4]{0:T(128)S(1)}, s32[4]{0:T(128)}, u32[]{:S(2)}) copy-start(s32[4]{0:T(128)} %param.11) | copy-start | bytes 52
  46.0 211.6 %all-gather.11.cloned.1.call-start = ((), (), s32[]{:S(2)}) async-start(), calls=%async_computation.13 | async-start | bytes 9830400 | tf_op jit(solution)/shard_map/all_gather | solution.py:224
  47.6 38.2 %all-to-all-start = ((bf16[192,4,640]{2,0,1:T(8,128)(2,1)}), bf16[192,4,640]{2,0,1:T(8,128)(2,1)S(1)}, u32[]{:S(2)}, u32[]{:S(2)}) async-start(bf16[192,4,640]{2,0,1:T(8,128)(2,1)} %bitcast.58), calls=%async_computation | async-start | bytes 1966080 | tf_op jit(solution)/shard_map/all_to_all | solution.py:215
  51.8 276.8 %reduce-scatter.4.cloned.1.call-start = ((), (), s32[]{:S(2)}) async-start(), calls=%async_computation.10 | async-start | bytes 9830400 | tf_op jit(solution)/shard_map/reduce_scatter | solution.py:229
  84.5 12.8 %copy-start.1 = (bf16[3072,128]{1,0:T(8,128)(2,1)}, bf16[3072,128]{1,0:T(8,128)(2,1)S(1)}, u32[]{:S(2)}) copy-start(bf16[3072,128]{1,0:T(8,128)(2,1)S(1)} %get-tuple-element.15.k_ref) | copy-start | bytes 2359300
  85.8 1.1 copy-start.4
  97.4 0.9 copy-start.5
  213.3 1.4 copy-start.7
  213.3 152.7 %reduce-scatter.8.cloned.1.call-start = ((), (), s32[]{:S(2)}) async-start(), calls=%async_computation.14 | async-start | bytes 1966080 | tf_op jit(solution)/shard_map/reduce_scatter | solution.py:232
  257.6 10.6 %copy-start.2 = (bf16[3072,128]{1,0:T(8,128)(2,1)S(1)}, bf16[3072,128]{1,0:T(8,128)(2,1)}, u32[]{:S(2)}) copy-start(bf16[3072,128]{1,0:T(8,128)(2,1)} %copy-done.1) | copy-start | bytes 2359300
  257.6 10.6 %copy-start.3 = (bf16[128,3072]{1,0:T(8,128)(2,1)S(1)}, bf16[128,3072]{1,0:T(8,128)(2,1)}, u32[]{:S(2)}) copy-start(bf16[128,3072]{1,0:T(8,128)(2,1)} %copy.40.kt_ref) | copy-start | bytes 2359300
  257.6 10.7 %copy-start.6 = (bf16[768,640]{1,0:T(8,128)(2,1)S(1)}, bf16[768,640]{1,0:T(8,128)(2,1)}, u32[]{:S(2)}) copy-start(bf16[768,640]{1,0:T(8,128)(2,1)} %copy-done.5) | copy-start | bytes 2949124
  277.7 120.8 %reduce-scatter.6.cloned.1.call-start = ((), (), s32[]{:S(2)}) async-start(), calls=%async_computation.11 | async-start | bytes 2949120 | tf_op jit(solution)/shard_map/reduce_scatter | solution.py:230
  366.0 10.9 %all-to-all-start.4 = ((bf16[4,192,256]{2,1,0:T(8,128)(2,1)}), bf16[4,192,256]{2,1,0:T(8,128)(2,1)S(1)}, u32[]{:S(2)}, u32[]{:S(2)}) async-start(bf16[4,192,256]{2,1,0:T(8,128)(2,1)} %bitcast.74), calls=%async_computation.7 | async-start | bytes 786432 | tf_op jit(solution)/shard_map/all_to_all | solution.py:215
Sparse Core Ops, SparseCore 0:
  9.6 33.7 all-gather.8
  44.9 36.9 all-gather.4
  83.5 118.8 all-gather.6
  203.8 53.7 all-gather.10
  260.0 68.5 reduce-scatter.3
  330.8 35.1 reduce-scatter.7
  368.9 29.4 reduce-scatter.5

commit v2 on v1

v2 whole, which is shorter than its diff:
```python
import functools
import math

import jax
import jax.numpy as jnp
from jax import lax
from jax.experimental import pallas as pl
from jax.experimental.pallas import tpu as pltpu
from jax.sharding import Mesh, PartitionSpec as P

H = 40
KVH = 8
HD = 128
BLK = 128
NRESP = 4
G = H // KVH
KB = 256
NEG = -1e30
SCALE = 1.0 / math.sqrt(HD)
C2 = SCALE * math.log2(math.e)
NT = (((1,), (1,)), ((), ()))
NN = (((1,), (0,)), ((), ()))


def dot(a, b, dims=NN):
    return lax.dot_general(a, b, dims, preferred_element_type=jnp.float32)


def seg_start(info, pos, prompt):
    start = jnp.where(pos >= info[1], info[1], prompt)
    start = jnp.where(pos >= info[2], info[2], start)
    return jnp.where(pos >= info[3], info[3], start)


def block_range(q_first, q_rows, prompt):
    full = jnp.minimum(prompt, q_first + 1) // KB
    return full, (q_first + q_rows - 1) // KB + 1


def visible(info, q_first, q_rows, k_first, prompt):
    q_pos = q_first + lax.broadcasted_iota(jnp.int32, (1, q_rows), 1)
    start = seg_start(info, q_pos, prompt)
    k_pos = k_first + lax.broadcasted_iota(jnp.int32, (KB, q_rows), 0)
    return (k_pos <= q_pos) & ((k_pos < prompt) | (k_pos >= start))


def place():
    me = lax.axis_index("tg"), lax.axis_index("hd"), lax.axis_index("kv")
    return [x.astype(jnp.int32) for x in me]


def sizes():
    return lax.axis_size("tg"), lax.axis_size("hd"), lax.axis_size("kv")


def span(index, size):
    return pl.ds(pl.multiple_of(index * size, size), size)


def remote(src, dst, sems, slot, target):
    return pltpu.make_async_remote_copy(
        src_ref=src,
        dst_ref=dst,
        send_sem=sems.at[0, slot],
        recv_sem=sems.at[1, slot],
        device_id=target,
        device_id_type=pl.DeviceIdType.MESH,
    )


def greet():
    t, i, k = place()
    tg, hd, kv = sizes()
    barrier = pltpu.get_barrier_semaphore()
    c = t * hd + i
    for d in range(1, tg * hd):
        p = lax.rem(c + d, tg * hd)
        pl.semaphore_signal(barrier, inc=1, device_id=(p // hd, lax.rem(p, hd), k), device_id_type=pl.DeviceIdType.MESH)
    for e in range(1, kv):
        for j in range(hd):
            pl.semaphore_signal(
                barrier, inc=1, device_id=(t, lax.rem(i + j, hd), lax.rem(k + e, kv)), device_id_type=pl.DeviceIdType.MESH
            )
    pl.semaphore_wait(barrier, tg * hd - 1 + (kv - 1) * hd)


def plane_peer(d):
    t, i, k = place()
    _, hd, kv = sizes()
    share = 2 if hd % 2 == 0 else 1
    chips = hd // share
    core = lax.rem(i, share)
    p = lax.rem(k * chips + i // share + d + chips * kv, chips * kv)
    return lax.rem(p, chips) * share + core, p // chips


def gather_kernel(prompt, qb, info_ref, kv_ref, q_ref, wt_ref, gy_ref,
                  kvall_ref, qall_ref, wtall_ref, gyall_ref, o_ref, lse_ref,
                  vt_ref, m_ref, l_ref, acc_ref, kv_sem, q_sem, w_sem, g_sem, f_sem, own_sem):
    t, i, k = place()
    tg, hd, n_kv = sizes()
    tok = q_ref.shape[0]
    wide = q_ref.shape[1]
    wrows = wt_ref.shape[0]
    n = tg * hd
    c = t * hd + i
    share = 2 if hd % 2 == 0 else 1
    ring = hd // share * n_kv
    greet()

    def at(p):
        return p // hd, lax.rem(p, hd)

    own = [
        pltpu.make_async_copy(kv_ref.at[:, span(i, 2 * HD)], kvall_ref.at[span(c, tok), :], own_sem.at[0]),
        pltpu.make_async_copy(q_ref.at[:, span(i, G * HD)], qall_ref.at[span(i, tok), :], own_sem.at[1]),
        pltpu.make_async_copy(wt_ref.at[:, span(i, G * HD)], wtall_ref.at[span(c, wrows), :], own_sem.at[2]),
        pltpu.make_async_copy(gy_ref, gyall_ref.at[span(i, tok), span(k, wide)], own_sem.at[3]),
    ]
    for copy in own:
        copy.start()

    def kv_copy(d, to):
        tt, ii = at(lax.rem(c + d, n))
        src = c if to else lax.rem(c - d + n, n)
        return remote(kv_ref.at[:, span(ii, 2 * HD)], kvall_ref.at[span(src, tok), :], kv_sem, d, (tt, ii, k))

    def q_copy(d, to):
        ii = lax.rem(i + d, hd)
        src = i if to else lax.rem(i - d + hd, hd)
        return remote(q_ref.at[:, span(ii, G * HD)], qall_ref.at[span(src, tok), :], q_sem, d, (t, ii, k))

    def w_copy(d, to):
        tt, ii = at(lax.rem(c + d, n))
        src = c if to else lax.rem(c - d + n, n)
        return remote(wt_ref.at[:, span(ii, G * HD)], wtall_ref.at[span(src, wrows), :], w_sem, d, (tt, ii, k))

    def g_copy(d, to):
        ii, kk = plane_peer(d)
        si, sk = (i, k) if to else plane_peer(-d)
        return remote(gy_ref, gyall_ref.at[span(si, tok), span(sk, wide)], g_sem, d, (t, ii, kk))

    def f_copy(d, to):
        si, sk = plane_peer(-d)
        if not to:
            si = si + 1 - 2 * lax.rem(si, 2)
        block = gyall_ref.at[span(si, tok), span(sk, wide)]
        return remote(gy_ref if d == 0 else block, block, f_sem, d, (t, i + 1 - 2 * lax.rem(i, 2), k))

    for d in range(1, n):
        kv_copy(d, True).start()
    for d in range(1, hd):
        q_copy(d, True).start()
    for d in range(1, ring):
        g_copy(d, True).start()
    if share == 2:
        f_copy(0, True).start()
    for d in range(1, n):
        w_copy(d, True).start()

    own[0].wait()
    own[1].wait()
    for d in range(1, n):
        kv_copy(d, False).wait_recv()
    for d in range(1, hd):
        q_copy(d, False).wait_recv()

    def turn(b, carry):
        keys = span(b, KB)
        vt_ref[:, keys] = kvall_ref[keys, HD:].T
        return carry

    lax.fori_loop(0, kvall_ref.shape[0] // KB, turn, 0)
    fwd_body(prompt, qb, info_ref, qall_ref, kvall_ref, vt_ref, o_ref, lse_ref, m_ref, l_ref, acc_ref)

    for d in range(1, ring):
        g_copy(d, False).wait_recv()
        if share == 2:
            f_copy(d, True).start()
    for d in range(1, n):
        w_copy(d, False).wait_recv()
    if share == 2:
        for d in range(ring):
            f_copy(d, False).wait_recv()
            f_copy(d, True).wait_send()
    for d in range(1, n):
        kv_copy(d, True).wait_send()
        w_copy(d, True).wait_send()
    for d in range(1, hd):
        q_copy(d, True).wait_send()
    for d in range(1, ring):
        g_copy(d, True).wait_send()
    own[2].wait()
    own[3].wait()


def scatter_kernel(prompt, qb, info_ref, y_ref, q_ref, kv_ref, o_ref, lse_ref, do_ref,
                   yout_ref, dqout_ref, dkout_ref, dvout_ref,
                   pair_ref, yin_ref, dq_ref, dkv_ref, dkvin_ref, kt_ref, qs_ref, dos_ref, del_ref, p_ref, ds_ref,
                   dqt_ref, dk_ref, dv_ref, pair_sem, y_sem, dq_sem, dkv_sem, own_sem):
    t, i, k = place()
    tg, hd, n_kv = sizes()
    tok, wide = yout_ref.shape
    n = tg * hd
    c = t * hd + i
    share = 2 if hd % 2 == 0 else 1
    ring = hd // share * n_kv
    greet()
    other = i + 1 - 2 * lax.rem(i, 2)

    def pair_copy(d):
        ii, kk = plane_peer(d)
        ii = ii + 1 - 2 * lax.rem(ii, 2)
        return remote(y_ref.at[span(ii, tok), span(kk, wide)], pair_ref.at[d], pair_sem, d, (t, other, k))

    def y_copy(d):
        ii, kk = plane_peer(d)
        src = pair_ref.at[d] if share == 2 else y_ref.at[span(ii, tok), span(kk, wide)]
        return remote(src, yin_ref.at[d], y_sem, d, (t, ii, kk))

    if share == 2:
        for d in range(ring):
            pair_copy(d).start()
    else:
        for d in range(1, ring):
            y_copy(d).start()

    def turn(b, carry):
        keys = span(b, KB)
        kt_ref[:, keys] = kv_ref[keys, :HD].T
        return carry

    lax.fori_loop(0, kv_ref.shape[0] // KB, turn, 0)

    if share == 2:
        for d in [*range(1, ring), 0]:
            pair_copy(d).wait_recv()
            ii, kk = plane_peer(d)

            def add(r, carry):
                rows = span(r, 16)
                mine = y_ref[pl.ds(pl.multiple_of(ii * tok + r * 16, 16), 16), span(kk, wide)]
                pair_ref[d, rows, :] = (pair_ref[d, rows, :].astype(jnp.float32) + mine.astype(jnp.float32)).astype(jnp.bfloat16)
                return carry

            lax.fori_loop(0, tok // 16, add, 0)
            if d:
                y_copy(d).start()

    bwd_body(prompt, qb, info_ref, q_ref, kv_ref, kt_ref, o_ref, lse_ref, do_ref,
             dq_ref, dkv_ref, qs_ref, dos_ref, del_ref, p_ref, ds_ref, dqt_ref, dk_ref, dv_ref)

    def dkv_copy(d, to):
        p = lax.rem(c + d, n)
        src = c if to else lax.rem(c - d + n, n)
        return remote(dkv_ref.at[span(p, tok), :], dkvin_ref.at[src], dkv_sem, d, (p // hd, lax.rem(p, hd), k))

    def dq_copy(d, to):
        ii = lax.rem(i + d, hd)
        src = i if to else lax.rem(i - d + hd, hd)
        return remote(dq_ref.at[span(ii, tok), :], dqout_ref.at[:, span(src, G * HD)], dq_sem, d, (t, ii, k))

    for d in range(1, n):
        dkv_copy(d, True).start()
    for d in range(1, hd):
        dq_copy(d, True).start()
    own = [
        pltpu.make_async_copy(dkv_ref.at[span(c, tok), :], dkvin_ref.at[c], own_sem.at[0]),
        pltpu.make_async_copy(dq_ref.at[span(i, tok), :], dqout_ref.at[:, span(i, G * HD)], own_sem.at[1]),
    ]
    for copy in own:
        copy.start()

    for d in range(1, ring):
        y_copy(d).wait_recv()

    def y_sum(r, carry):
        rows = span(r, 16)
        if share == 2:
            total = pair_ref[0, rows, :].astype(jnp.float32)
        else:
            total = y_ref[pl.ds(pl.multiple_of(i * tok + r * 16, 16), 16), span(k, wide)].astype(jnp.float32)
        for d in range(1, ring):
            total += yin_ref[d, rows, :].astype(jnp.float32)
        yout_ref[rows, :] = total.astype(jnp.bfloat16)
        return carry

    lax.fori_loop(0, tok // 16, y_sum, 0)
    own[0].wait()
    own[1].wait()
    for d in range(1, n):
        dkv_copy(d, False).wait_recv()

    def kv_sum(r, carry):
        rows = span(r, 32)
        for j in range(hd):
            total = dkvin_ref[j, rows, :].astype(jnp.float32)
            for u in range(1, tg):
                total += dkvin_ref[u * hd + j, rows, :].astype(jnp.float32)
            cols = slice(j * HD, (j + 1) * HD)
            dkout_ref[rows, cols] = total[:, :HD].astype(jnp.bfloat16)
            dvout_ref[rows, cols] = total[:, HD:].astype(jnp.bfloat16)
        return carry

    lax.fori_loop(0, tok // 32, kv_sum, 0)
    for d in range(1, hd):
        dq_copy(d, False).wait_recv()
        dq_copy(d, True).wait_send()
    for d in range(1, n):
        dkv_copy(d, True).wait_send()
    for d in range(1, ring):
        y_copy(d).wait_send()
    if share == 2:
        for d in range(ring):
            pair_copy(d).wait_send()


def read_info(info_ref):
    return [info_ref[i] for i in range(4)]


def fwd_body(prompt, qb, info_ref, q_ref, kv_ref, vt_ref, o_ref, lse_ref, m_ref, l_ref, acc_ref):
    info = read_info(info_ref)
    first_row = lax.axis_index("tg").astype(jnp.int32) * q_ref.shape[0]
    blocks = q_ref.shape[0] // qb

    def query_block(i, carry):
        rows = pl.ds(pl.multiple_of(i * qb, qb), qb)
        q_first = first_row + i * qb
        m_ref[...] = jnp.full_like(m_ref, NEG)
        l_ref[...] = jnp.zeros_like(l_ref)
        acc_ref[...] = jnp.zeros_like(acc_ref)
        full, last = block_range(q_first, qb, prompt)

        def key_block(masked, b, carry):
            keys = pl.ds(pl.multiple_of(b * KB, KB), KB)
            k_blk = kv_ref[keys, :HD]
            vt_blk = vt_ref[:, keys]
            vis = visible(info, q_first, qb, b * KB, prompt) if masked else None
            for h in range(G):
                s = dot(k_blk, q_ref[rows, h * HD:(h + 1) * HD], NT) * C2
                if masked:
                    s = jnp.where(vis, s, NEG)
                m_old = m_ref[h:h + 1, :]
                m_new = jnp.maximum(m_old, jnp.max(s, axis=0, keepdims=True))
                p = jnp.exp2(s - m_new)
                alpha = jnp.exp2(m_old - m_new)
                m_ref[h:h + 1, :] = m_new
                l_ref[h:h + 1, :] = l_ref[h:h + 1, :] * alpha + jnp.sum(p, axis=0, keepdims=True)
                acc_ref[h] = acc_ref[h] * alpha + dot(vt_blk, p.astype(jnp.bfloat16))
            return carry

        lax.fori_loop(0, full, functools.partial(key_block, False), 0)
        lax.fori_loop(full, last, functools.partial(key_block, True), 0)
        for h in range(G):
            l = l_ref[h:h + 1, :]
            o_ref[rows, h * HD:(h + 1) * HD] = (acc_ref[h] / l).T.astype(jnp.bfloat16)
            lse_ref[i, h:h + 1, :] = m_ref[h:h + 1, :] + jnp.log2(l)
        return carry

    lax.fori_loop(0, blocks, query_block, 0)


def bwd_body(prompt, qb, info_ref, q_ref, kv_ref, kt_ref, o_ref, lse_ref, do_ref,
               dq_ref, dkv_ref, qs_ref, dos_ref, del_ref, p_ref, ds_ref, dqt_ref, dk_ref, dv_ref):
    info = read_info(info_ref)
    first_row = lax.axis_index("tg").astype(jnp.int32) * q_ref.shape[0]
    blocks = q_ref.shape[0] // qb
    dk_ref[...] = jnp.zeros_like(dk_ref)
    dv_ref[...] = jnp.zeros_like(dv_ref)

    def query_block(i, carry):
        rows = pl.ds(pl.multiple_of(i * qb, qb), qb)
        q_first = first_row + i * qb
        for h in range(G):
            cols = slice(h * HD, (h + 1) * HD)
            do = do_ref[rows, cols]
            qs_ref[h * qb:(h + 1) * qb, :] = q_ref[rows, cols]
            dos_ref[h * qb:(h + 1) * qb, :] = do
            prod = do.astype(jnp.float32) * o_ref[rows, cols].astype(jnp.float32)
            del_ref[h:h + 1, :] = jnp.sum(prod.T, axis=0, keepdims=True)
        dqt_ref[...] = jnp.zeros_like(dqt_ref)
        full, last = block_range(q_first, qb, prompt)

        def key_block(masked, b, carry):
            keys = pl.ds(pl.multiple_of(b * KB, KB), KB)
            k_blk = kv_ref[keys, :HD]
            v_blk = kv_ref[keys, HD:]
            vis = visible(info, q_first, qb, b * KB, prompt) if masked else None
            for h in range(G):
                part = slice(h * qb, (h + 1) * qb)
                s = dot(k_blk, qs_ref[part, :], NT) * C2
                p = jnp.exp2(s - lse_ref[i, h:h + 1, :])
                if masked:
                    p = jnp.where(vis, p, 0.0)
                dp = dot(v_blk, dos_ref[part, :], NT)
                p_ref[h] = p.astype(jnp.bfloat16)
                ds_ref[h] = (p * (dp - del_ref[h:h + 1, :])).astype(jnp.bfloat16)
            dv = jnp.zeros((KB, HD), jnp.float32)
            dk = jnp.zeros((KB, HD), jnp.float32)
            for h in range(G):
                part = slice(h * qb, (h + 1) * qb)
                dv += dot(p_ref[h], dos_ref[part, :])
                dk += dot(ds_ref[h], qs_ref[part, :])
                dqt_ref[h] += dot(kt_ref[:, keys], ds_ref[h])
            dv_ref[keys, :] += dv
            dk_ref[keys, :] += dk
            return carry

        lax.fori_loop(0, full, functools.partial(key_block, False), 0)
        lax.fori_loop(full, last, functools.partial(key_block, True), 0)
        for h in range(G):
            dq_ref[rows, h * HD:(h + 1) * HD] = (dqt_ref[h] * SCALE).T.astype(jnp.bfloat16)
        return carry

    lax.fori_loop(0, blocks, query_block, 0)
    dkv_ref[:, :HD] = (dk_ref[...] * SCALE).astype(jnp.bfloat16)
    dkv_ref[:, HD:] = dv_ref[...].astype(jnp.bfloat16)


VM = pl.BlockSpec(memory_space=pltpu.VMEM)
SM = pl.BlockSpec(memory_space=pltpu.SMEM)
ANY = pl.BlockSpec(memory_space=pl.ANY)
BF = jnp.bfloat16
F32 = jnp.float32


def dma(count):
    return pltpu.SemaphoreType.DMA((2, count))


def gather_and_forward(info, kv, q, wt, gy, prompt, qb):
    tg, hd, n_kv = sizes()
    tok, n = q.shape[0], tg * hd
    rows, keys = tok * hd, tok * n
    work = G * rows * keys
    shape = jax.ShapeDtypeStruct
    return pl.pallas_call(
        functools.partial(gather_kernel, prompt, qb),
        out_shape=(
            shape((keys, 2 * HD), BF),
            shape((rows, G * HD), BF),
            shape((wt.shape[0] * n, G * HD), BF),
            shape((rows, gy.shape[1] * n_kv), BF),
            shape((rows, G * HD), BF),
            shape((rows // qb, 8, qb), F32),
        ),
        in_specs=[SM, ANY, ANY, ANY, ANY],
        out_specs=(VM, VM, ANY, ANY, VM, VM),
        scratch_shapes=[
            pltpu.VMEM((HD, keys), BF),
            pltpu.VMEM((8, qb), F32),
            pltpu.VMEM((8, qb), F32),
            pltpu.VMEM((G, HD, qb), F32),
            dma(n), dma(hd), dma(n), dma(hd * n_kv), dma(hd * n_kv),
            pltpu.SemaphoreType.DMA((4,)),
        ],
        compiler_params=pltpu.CompilerParams(vmem_limit_bytes=40 << 20, collective_id=0, has_side_effects=True),
        cost_estimate=pl.CostEstimate(flops=work * HD * 4, bytes_accessed=32 << 20, transcendentals=work),
        name="gather_and_forward",
    )(info, kv, q, wt, gy)


def backward_and_scatter(info, y, q, kv, o, lse, do, tok, wide, prompt, qb):
    tg, hd, n_kv = sizes()
    n = tg * hd
    rows, keys = tok * hd, tok * n
    share = 2 if hd % 2 == 0 else 1
    ring = hd // share * n_kv
    work = G * rows * keys
    shape = jax.ShapeDtypeStruct
    return pl.pallas_call(
        functools.partial(scatter_kernel, prompt, qb),
        out_shape=(
            shape((tok, wide), BF),
            shape((tok, hd * G * HD), BF),
            shape((tok, hd * HD), BF),
            shape((tok, hd * HD), BF),
        ),
        in_specs=[SM] + [VM] * 6,
        out_specs=(VM,) * 4,
        scratch_shapes=[
            pltpu.VMEM((ring if share == 2 else 1, tok, wide), BF),
            pltpu.VMEM((ring, tok, wide), BF),
            pltpu.VMEM((rows, G * HD), BF),
            pltpu.VMEM((keys, 2 * HD), BF),
            pltpu.VMEM((n, tok, 2 * HD), BF),
            pltpu.VMEM((HD, keys), BF),
            pltpu.VMEM((G * qb, HD), BF),
            pltpu.VMEM((G * qb, HD), BF),
            pltpu.VMEM((8, qb), F32),
            pltpu.VMEM((G, KB, qb), BF),
            pltpu.VMEM((G, KB, qb), BF),
            pltpu.VMEM((G, HD, qb), F32),
            pltpu.VMEM((keys, HD), F32),
            pltpu.VMEM((keys, HD), F32),
            dma(ring), dma(ring), dma(hd), dma(n),
            pltpu.SemaphoreType.DMA((2,)),
        ],
        compiler_params=pltpu.CompilerParams(vmem_limit_bytes=56 << 20, collective_id=1, has_side_effects=True),
        cost_estimate=pl.CostEstimate(flops=work * HD * 10, bytes_accessed=32 << 20, transcendentals=work),
        name="backward_and_scatter",
    )(info, y, q, kv, o, lse, do)


def local(queries, keys, values, w_out, grad_y, resp_blocks):
    heads = lax.axis_size("hd")
    tok = queries.shape[0]
    rows = tok * heads
    prompt = rows * lax.axis_size("tg") // 2
    qb = 256 if rows % 256 == 0 else rows
    ends = prompt + jnp.cumsum(resp_blocks[: NRESP - 1]).astype(jnp.int32) * BLK
    info = jnp.concatenate([jnp.zeros((1,), jnp.int32), ends])
    kv = jnp.concatenate([keys.reshape(tok, heads, HD), values.reshape(tok, heads, HD)], axis=2)
    kv = kv.reshape(tok, heads * 2 * HD)
    kv_all, q, wt, gy, attn, lse = gather_and_forward(info, kv, queries, w_out.T, grad_y, prompt, qb)
    y = dot(attn, wt, NT).astype(BF)
    grad_attn = dot(gy, wt).astype(BF)
    return backward_and_scatter(info, y, q, kv_all, attn, lse, grad_attn, tok, grad_y.shape[1], prompt, qb)


def solution(mesh):
    ctx, n_kv = mesh.devices.shape
    heads = KVH // n_kv
    split = Mesh(mesh.devices.reshape(ctx // heads, heads, n_kv), ("tg", "hd", "kv"))
    tok = ("tg", "hd")
    tiled = P(tok, "kv")
    return jax.shard_map(
        local,
        mesh=split,
        in_specs=(tiled, tiled, tiled, P("kv", tok), tiled, P()),
        out_specs=(tiled,) * 4,
        check_vma=False,
    )
```

time: 407 us -> 302 us (0.74)
  waiting for transfers between devices: 273 us -> 0 us
  Pallas kernels: 19.8 us -> 268 us
  blocking collectives: 51.3 us -> 0 us
  between operations: 14.3 us -> 0.74 us
  starting transfers between devices: 8.91 us -> 0 us
    pallas_call x2, Pallas kernels: 19.8 us -> 268 us  [the longest x1 148 us: gather_and_forward(): pl.pallas_call(functools.partial(gather_kernel, prompt, qb), out_shape=(s...]
    all_gather x4 -> x0, waiting for transfers between devices: 176 us -> none  [the longest x1 104 us: local(): wt = lax.all_gather(wt, 'tg', axis=0, tiled=True)]
    reduce_scatter x3 -> x0, waiting for transfers between devices: 90.8 us -> none  [the longest x1 50.8 us: local(): y = lax.psum_scatter(y, 'hd', scatter_dimension=0, tiled=True)]
    all_to_all x3 -> x0, blocking collectives: 51.3 us -> none  [a2a(): lax.all_to_all(x, 'hd', split, concat, tiled=True)]
    dot_general x1 -> x0, matrix products: 10.6 us -> none  [local(): jnp.dot(gy, wt, preferred_element_type=jnp.float32).astype(jnp.bfloat16)]
    all_to_all x2 -> x0, starting transfers between devices: 8.49 us -> none  [a2a(): lax.all_to_all(x, 'hd', split, concat, tiled=True)]
    dot_general x1 -> x2, matrix products: 10.9 us -> 19 us  [dot(): return lax.dot_general(a, b, dims, preferred_element_type=jnp.float32)]
    unnamed x24 -> x21, local copies, waits for them, and re-layouts: 5.27 us -> 11.6 us
  transfers between devices with their start and end apart: 9 -> 0, of which waited for: 7 -> 0; matrix products, arithmetic and copies ran while one was open for 8% -> 0% of each run, Pallas kernels for 5% -> 0%
where the time goes in v2:
time: 302 us
  Pallas kernels  268 us (89%)
  matrix products  19 us (6%)
  local copies, waits for them, and re-layouts  14.2 us (5%)
    pallas_call x1, Pallas kernels, gather_and_forward(): pl.pallas_call(functools.partial(gather_kernel, prompt, qb), out_shape=(s...  148 us
    pallas_call x1, Pallas kernels, backward_and_scatter(): pl.pallas_call(functools.partial(scatter_kernel, prompt, qb), out_shape=(...  119 us
    dot_general x2, matrix products, dot(): return lax.dot_general(a, b, dims, preferred_element_type=jnp.float32)  19 us
    unnamed x21, local copies, waits for them, and re-layouts  11.6 us

profile of v2, /device:TPU:1, one launch (start us, length us, event | category | flops | bytes accessed | tf_op | source)
XLA Modules:
  0.0 302.0 jit_solution(6463151559531385889)
XLA Ops:
  0.6 0.7 slice_bitcast_fusion
  1.3 0.2 reduce-window.9
  1.5 0.1 pad_add_fusion.info_ref
  1.6 1.0 reshape.46
  2.5 1.0 reshape.47
  3.5 0.2 pad_maximum_fusion
  3.7 0.1 copy.10
  3.8 0.0 copy-start
  3.8 1.4 copy-done
  5.2 1.2 copy-done.1
  6.4 1.2 copy-done.2
  7.6 148.5 %gather_and_forward.1 = (bf16[3072,256]{1,0:T(8,128)(2,1)S(1)}, bf16[768,640]{1,0:T(8,128)(2,1)S(1)}, bf16[5120,640]{1,0:T(8,128)(2,1)S(1)}, bf16[768,5120]{1,0:...) custom-call(s32[4]{0:T(128)S(1)} %pad_add_fusion.info_ref, bf16[192,1024]{1,0:T(8,128)(2,1)S(1)} %bitcast.11, ...), custom_call_target="tpu_custom_call" | custom-call | flops 6039797760 | bytes 33554432 | tf_op jit(solution)/shard_map/gather_and_forward/pallas_call | solution.py:438
  156.1 0.0 copy-done.3
  156.1 0.0 copy-start.4
  156.2 0.0 copy-start.6
  156.2 0.0 copy-start.7
  156.2 10.6 %convolution_convert_fusion.1.do_ref = bf16[768,640]{1,0:T(8,128)(2,1)} fusion(bf16[768,5120]{1,0:T(8,128)(2,1)} %get-tuple-element.15, bf16[5120,640]{1,0:T(8,128)(2,1)S(1)} %get-tuple-element.11), kind=kOutput, calls=%fused_computation.1 | convolution fusion | flops 5033656320 | bytes 15400960 | tf_op jit(solution)/shard_map/dot_general | solution.py:26
  166.7 0.0 copy-done.4
  166.8 8.5 %convolution_convert_fusion.y_ref = bf16[768,5120]{1,0:T(8,128)(2,1)} fusion(bf16[768,640]{1,0:T(8,128)(2,1)S(1)} %get-tuple-element.10.o_ref, bf16[5120,640]{1,0:T(8,128)(2,1)S(1)} %get-tuple-element.11), kind=kOutput, calls=%fused_computation | convolution fusion | flops 5037096960 | bytes 15400960 | tf_op jit(solution)/shard_map/dot_general | solution.py:26
  175.2 119.1 %backward_and_scatter.1 = (bf16[192,2560]{1,0:T(8,128)(2,1)}, bf16[192,2560]{1,0:T(8,128)(2,1)}, bf16[192,512]{1,0:T(8,128)(2,1)}, bf16[192,512]{1,0:T(8,128)(2,1)}) custom-call(s32[4]{0:T(128)} %copy-done.3, bf16[768,5120]{1,0:T(8,128)(2,1)} %convolution_convert_fusion.y_ref, bf16[768,640]{1,0:T(8,128)(2,1)} %copy-done.6, bf16[3072,256]{1,0:T(8,128)(2,1)} %copy-done.5, ...), custom_call_target="tpu_custom_call" | custom-call | flops 15099494400 | bytes 33554432 | tf_op jit(solution)/shard_map/backward_and_scatter/pallas_call | solution.py:472
  294.3 2.2 copy.15
  296.5 2.2 copy.16
  298.8 1.6 copy.17
  300.4 1.6 copy.18
  (8 shorter events, 0.0 us)
Async XLA Ops:
  1.6 154.6 %copy-start.3 = (s32[4]{0:T(128)}, s32[4]{0:T(128)S(1)}, u32[]{:S(2)}) copy-start(s32[4]{0:T(128)S(1)} %pad_add_fusion.info_ref) | copy-start | bytes 52
  3.8 1.4 copy-start
  5.2 1.2 copy-start.1
  6.4 1.2 copy-start.2
  156.1 10.6 %copy-start.4 = (bf16[768,640]{1,0:T(8,128)(2,1)}, bf16[768,640]{1,0:T(8,128)(2,1)S(1)}, u32[]{:S(2)}) copy-start(bf16[768,640]{1,0:T(8,128)(2,1)S(1)} %get-tuple-element.10.o_ref) | copy-start | bytes 2949124
  156.1 10.6 %copy-start.5 = (bf16[3072,256]{1,0:T(8,128)(2,1)}, bf16[3072,256]{1,0:T(8,128)(2,1)S(1)}, u32[]{:S(2)}) copy-start(bf16[3072,256]{1,0:T(8,128)(2,1)S(1)} %get-tuple-element.13.kv_ref) | copy-start | bytes 4718596
  156.2 10.6 %copy-start.6 = (bf16[768,640]{1,0:T(8,128)(2,1)}, bf16[768,640]{1,0:T(8,128)(2,1)S(1)}, u32[]{:S(2)}) copy-start(bf16[768,640]{1,0:T(8,128)(2,1)S(1)} %get-tuple-element.12.q_ref) | copy-start | bytes 2949124
  156.2 10.6 %copy-start.7 = (f32[3,8,256]{2,1,0:T(8,128)}, f32[3,8,256]{2,1,0:T(8,128)S(1)}, u32[]{:S(2)}) copy-start(f32[3,8,256]{2,1,0:T(8,128)S(1)} %get-tuple-element.14.lse_ref) | copy-start | bytes 73732

commit v3 on v2

--- a/solution.py
+++ b/solution.py
@@ -95,8 +95,9 @@
 
 
 def gather_kernel(prompt, qb, info_ref, kv_ref, q_ref, wt_ref, gy_ref,
-                  kvall_ref, qall_ref, wtall_ref, gyall_ref, o_ref, lse_ref,
-                  vt_ref, m_ref, l_ref, acc_ref, kv_sem, q_sem, w_sem, g_sem, f_sem, own_sem):
+                  kvall_ref, qall_ref, o_ref, lse_ref, y_ref, do_ref,
+                  wtall_ref, gyall_ref, ga_ref, vt_ref, m_ref, l_ref, acc_ref,
+                  kv_sem, q_sem, w_sem, first_up, first_down, up_sem, down_sem, g_sem, f_sem, own_sem):
     t, i, k = place()
     tg, hd, n_kv = sizes()
     tok = q_ref.shape[0]
@@ -131,9 +132,69 @@
         return remote(q_ref.at[:, span(ii, G * HD)], qall_ref.at[span(src, tok), :], q_sem, d, (t, ii, k))
 
     def w_copy(d, to):
-        tt, ii = at(lax.rem(c + d, n))
-        src = c if to else lax.rem(c - d + n, n)
-        return remote(wt_ref.at[:, span(ii, G * HD)], wtall_ref.at[span(src, wrows), :], w_sem, d, (tt, ii, k))
+        ii = lax.rem(i + d, hd)
+        src = i if to else lax.rem(i - d + hd, hd)
+        return remote(wt_ref.at[:, span(ii, G * HD)], wtall_ref.at[span(t * hd + src, wrows), :], w_sem, d, (t, ii, k))
+
+    def first_hop(d, step, to):
+        src = lax.rem(i - d + hd, hd)
+        rows = span((t if to else t - step) * hd + src, wrows)
+        block = wtall_ref.at[rows, :]
+        out = wt_ref.at[:, span(i, G * HD)] if d == 0 else block
+        return remote(out, block, first_up if step > 0 else first_down, d, (t + step, i, k))
+
+    def hop(h, step, to):
+        block = wtall_ref.at[span(t - step * (h if to else h + 1), wrows * hd), :]
+        return remote(block, block, up_sem if step > 0 else down_sem, h, (t + step, i, k))
+
+    def has(h, step):
+        return t >= h if step > 0 else t + h < tg
+
+    def more(step):
+        return t < tg - 1 if step > 0 else t > 0
+
+    def arrive_first():
+        for step in (1, -1):
+            @pl.when(has(1, step))
+            def _():
+                for d in range(hd):
+                    first_hop(d, step, False).wait_recv()
+
+            if tg > 2:
+                @pl.when(has(1, step) & more(step))
+                def _():
+                    hop(1, step, True).start()
+
+    def arrive(h):
+        for step in (1, -1):
+            @pl.when(has(h, step))
+            def _():
+                hop(h - 1, step, False).wait_recv()
+
+            @pl.when(has(h, step) & more(step) & (h < tg - 1))
+            def _():
+                hop(h, step, True).start()
+
+    part = wtall_ref.shape[0] // 4 if wrows * hd % HD else wrows * hd
+
+    def project(u):
+        cols = span(u, part)
+
+        def tile(r, carry):
+            rows = span(r, qb)
+            w = wtall_ref[cols, :]
+            ga_ref[rows, :] += dot(gyall_ref[rows, cols], w)
+            y_ref[rows, cols] = dot(o_ref[rows, :], w, NT).astype(BF)
+            return carry
+
+        lax.fori_loop(0, o_ref.shape[0] // qb, tile, 0)
+
+    def project_far(h):
+        if wrows * hd % HD == 0:
+            for step in (1, -1):
+                @pl.when(has(h, step))
+                def _():
+                    project(t - step * h)
 
     def g_copy(d, to):
         ii, kk = plane_peer(d)
@@ -150,14 +211,25 @@
     for d in range(1, n):
         kv_copy(d, True).start()
     for d in range(1, hd):
+        w_copy(d, True).start()
+    for d in range(1, hd):
         q_copy(d, True).start()
+    for step in (1, -1):
+        @pl.when(more(step))
+        def _():
+            first_hop(0, step, True).start()
     for d in range(1, ring):
         g_copy(d, True).start()
     if share == 2:
         f_copy(0, True).start()
-    for d in range(1, n):
-        w_copy(d, True).start()
-
+    for d in range(1, hd):
+        w_copy(d, False).wait_recv()
+        for step in (1, -1):
+            @pl.when(more(step))
+            def _():
+                first_hop(d, step, True).start()
+
+    ga_ref[...] = jnp.zeros_like(ga_ref)
     own[0].wait()
     own[1].wait()
     for d in range(1, n):
@@ -171,27 +243,57 @@
         return carry
 
     lax.fori_loop(0, kvall_ref.shape[0] // KB, turn, 0)
-    fwd_body(prompt, qb, info_ref, qall_ref, kvall_ref, vt_ref, o_ref, lse_ref, m_ref, l_ref, acc_ref)
+    blocks = o_ref.shape[0] // qb
+    fwd_body(prompt, qb, info_ref, qall_ref, kvall_ref, vt_ref, o_ref, lse_ref, m_ref, l_ref, acc_ref,
+             arrive_first, max(blocks - 2, 0))
 
     for d in range(1, ring):
         g_copy(d, False).wait_recv()
         if share == 2:
             f_copy(d, True).start()
-    for d in range(1, n):
-        w_copy(d, False).wait_recv()
     if share == 2:
         for d in range(ring):
             f_copy(d, False).wait_recv()
+    own[2].wait()
+    own[3].wait()
+    if wrows * hd % HD == 0:
+        project(t)
+
+    def step_far(h, carry):
+        arrive(h + 1)
+        project_far(h)
+        return carry
+
+    lax.fori_loop(1, tg - 1, step_far, 0)
+    project_far(tg - 1)
+    if wrows * hd % HD:
+        lax.fori_loop(0, 4, lambda u, carry: (project(u), carry)[1], 0)
+    do_ref[...] = ga_ref[...].astype(BF)
+
+    if share == 2:
+        for d in range(ring):
             f_copy(d, True).wait_send()
     for d in range(1, n):
         kv_copy(d, True).wait_send()
+    for d in range(1, hd):
         w_copy(d, True).wait_send()
-    for d in range(1, hd):
         q_copy(d, True).wait_send()
     for d in range(1, ring):
         g_copy(d, True).wait_send()
-    own[2].wait()
-    own[3].wait()
+    for step in (1, -1):
+        @pl.when(more(step))
+        def _():
+            for d in range(hd):
+                first_hop(d, step, True).wait_send()
+
+        def sent(h, carry):
+            @pl.when(has(h, step) & more(step))
+            def _():
+                hop(h, step, True).wait_send()
+
+            return carry
+
+        lax.fori_loop(1, tg - 1, sent, 0)
 
 
 def scatter_kernel(prompt, qb, info_ref, y_ref, q_ref, kv_ref, o_ref, lse_ref, do_ref,
@@ -319,7 +421,7 @@
     return [info_ref[i] for i in range(4)]
 
 
-def fwd_body(prompt, qb, info_ref, q_ref, kv_ref, vt_ref, o_ref, lse_ref, m_ref, l_ref, acc_ref):
+def fwd_body(prompt, qb, info_ref, q_ref, kv_ref, vt_ref, o_ref, lse_ref, m_ref, l_ref, acc_ref, between, after):
     info = read_info(info_ref)
     first_row = lax.axis_index("tg").astype(jnp.int32) * q_ref.shape[0]
     blocks = q_ref.shape[0] // qb
@@ -356,6 +458,7 @@
             l = l_ref[h:h + 1, :]
             o_ref[rows, h * HD:(h + 1) * HD] = (acc_ref[h] / l).T.astype(jnp.bfloat16)
             lse_ref[i, h:h + 1, :] = m_ref[h:h + 1, :] + jnp.log2(l)
+        pl.when(i == after)(between)
         return carry
 
     lax.fori_loop(0, blocks, query_block, 0)
@@ -440,22 +543,25 @@
         out_shape=(
             shape((keys, 2 * HD), BF),
             shape((rows, G * HD), BF),
-            shape((wt.shape[0] * n, G * HD), BF),
+            shape((rows, G * HD), BF),
+            shape((rows // qb, 8, qb), F32),
             shape((rows, gy.shape[1] * n_kv), BF),
             shape((rows, G * HD), BF),
-            shape((rows // qb, 8, qb), F32),
         ),
         in_specs=[SM, ANY, ANY, ANY, ANY],
-        out_specs=(VM, VM, ANY, ANY, VM, VM),
+        out_specs=(VM,) * 6,
         scratch_shapes=[
+            pltpu.VMEM((wt.shape[0] * n, G * HD), BF),
+            pltpu.VMEM((rows, gy.shape[1] * n_kv), BF),
+            pltpu.VMEM((rows, G * HD), F32),
             pltpu.VMEM((HD, keys), BF),
             pltpu.VMEM((8, qb), F32),
             pltpu.VMEM((8, qb), F32),
             pltpu.VMEM((G, HD, qb), F32),
-            dma(n), dma(hd), dma(n), dma(hd * n_kv), dma(hd * n_kv),
+            dma(n), dma(hd), dma(hd), dma(hd), dma(hd), dma(tg), dma(tg), dma(hd * n_kv), dma(hd * n_kv),
             pltpu.SemaphoreType.DMA((4,)),
         ],
-        compiler_params=pltpu.CompilerParams(vmem_limit_bytes=40 << 20, collective_id=0, has_side_effects=True),
+        compiler_params=pltpu.CompilerParams(vmem_limit_bytes=56 << 20, collective_id=0, has_side_effects=True),
         cost_estimate=pl.CostEstimate(flops=work * HD * 4, bytes_accessed=32 << 20, transcendentals=work),
         name="gather_and_forward",
     )(info, kv, q, wt, gy)
@@ -513,9 +619,7 @@
     info = jnp.concatenate([jnp.zeros((1,), jnp.int32), ends])
     kv = jnp.concatenate([keys.reshape(tok, heads, HD), values.reshape(tok, heads, HD)], axis=2)
     kv = kv.reshape(tok, heads * 2 * HD)
-    kv_all, q, wt, gy, attn, lse = gather_and_forward(info, kv, queries, w_out.T, grad_y, prompt, qb)
-    y = dot(attn, wt, NT).astype(BF)
-    grad_attn = dot(gy, wt).astype(BF)
+    kv_all, q, attn, lse, y, grad_attn = gather_and_forward(info, kv, queries, w_out.T, grad_y, prompt, qb)
     return backward_and_scatter(info, y, q, kv_all, attn, lse, grad_attn, tok, grad_y.shape[1], prompt, qb)
 
 

time: 302 us -> 258 us (0.85)
  Pallas kernels: 268 us -> 248 us
  matrix products: 19 us -> 0 us
  local copies, waits for them, and re-layouts: 14.2 us -> 8.04 us
    pallas_call x1, Pallas kernels: 119 us -> 86.4 us  [backward_and_scatter(): pl.pallas_call(functools.partial(scatter_kernel, prompt, qb), out_shape=(...]
    dot_general x2 -> x0, matrix products: 19 us -> none  [dot(): return lax.dot_general(a, b, dims, preferred_element_type=jnp.float32)]
    pallas_call x1, Pallas kernels: 148 us -> 162 us  [gather_and_forward(): pl.pallas_call(functools.partial(gather_kernel, prompt, qb), out_shape=(s...]
    unnamed x21 -> x11, local copies, waits for them, and re-layouts: 11.6 us -> 5.42 us
where the time goes in v3:
time: 258 us
  Pallas kernels  248 us (96%)
  local copies, waits for them, and re-layouts  8.04 us (3%)
    pallas_call x1, Pallas kernels, gather_and_forward(): pl.pallas_call(functools.partial(gather_kernel, prompt, qb), out_shape=(s...  162 us
    pallas_call x1, Pallas kernels, backward_and_scatter(): pl.pallas_call(functools.partial(scatter_kernel, prompt, qb), out_shape=(...  86.4 us
    unnamed x11, local copies, waits for them, and re-layouts  5.42 us

profile of v3, /device:TPU:1, one launch (start us, length us, event | category | flops | bytes accessed | tf_op | source)
XLA Modules:
  0.0 258.2 jit_solution(14437374761909372272)
XLA Ops:
  0.6 0.7 slice_bitcast_fusion
  1.3 0.2 reduce-window.9
  1.5 0.6 pad_add_fusion.info_ref
  2.1 1.0 reshape.46
  3.0 1.0 reshape.47
  4.0 0.2 pad_maximum_fusion
  4.2 0.8 copy.10
  5.0 162.0 %gather_and_forward.1 = (bf16[3072,256]{1,0:T(8,128)(2,1)}, bf16[768,640]{1,0:T(8,128)(2,1)}, bf16[768,640]{1,0:T(8,128)(2,1)}, f32[3,8,256]{2,1,0:T(8,128)}, bf...) custom-call(s32[4]{0:T(128)} %pad_add_fusion.info_ref, bf16[192,1024]{1,0:T(8,128)(2,1)} %bitcast.8, ...), custom_call_target="tpu_custom_call" | custom-call | flops 6039797760 | bytes 33554432 | tf_op jit(solution)/shard_map/gather_and_forward/pallas_call | solution.py:541
  167.1 86.4 %backward_and_scatter.1 = (bf16[192,2560]{1,0:T(8,128)(2,1)}, bf16[192,2560]{1,0:T(8,128)(2,1)}, bf16[192,512]{1,0:T(8,128)(2,1)}, bf16[192,512]{1,0:T(8,128)(2,1)}) custom-call(s32[4]{0:T(128)} %pad_add_fusion.info_ref, bf16[768,5120]{1,0:T(8,128)(2,1)} %get-tuple-element.10.y_ref, bf16[768,640]{1,0:T(8,128)(2,1)} %get-tuple-element.11.q_ref, ...), custom_call_target="tpu_custom_call" | custom-call | flops 15099494400 | bytes 33554432 | tf_op jit(solution)/shard_map/backward_and_scatter/pallas_call | solution.py:578
  253.5 0.0 copy-start
  253.6 0.0 copy-start.2
  253.6 2.3 copy.15
  255.9 0.0 copy-done
  255.9 0.0 copy-start.1
  255.9 0.9 copy.16
  256.8 0.0 copy-done.2
  256.8 0.7 copy.17
  257.5 0.0 copy-done.1
  257.5 0.7 copy.18
  (1 shorter events, 0.0 us)
Async XLA Ops:
  253.5 2.3 copy-start
  253.6 3.3 %copy-start.2 = (bf16[192,512]{1,0:T(8,128)(2,1)S(1)}, bf16[192,512]{1,0:T(8,128)(2,1)}, u32[]{:S(2)}) copy-start(bf16[192,512]{1,0:T(8,128)(2,1)} %get-tuple-element.22) | copy-start | bytes 589828
  255.9 1.6 copy-start.1

commit v4 on v3

--- a/solution.py
+++ b/solution.py
@@ -251,6 +251,8 @@
         g_copy(d, False).wait_recv()
         if share == 2:
             f_copy(d, True).start()
+    if tg > 2:
+        arrive(2)
     if share == 2:
         for d in range(ring):
             f_copy(d, False).wait_recv()
@@ -260,12 +262,13 @@
         project(t)
 
     def step_far(h, carry):
-        arrive(h + 1)
         project_far(h)
+        arrive(h + 2)
         return carry
 
-    lax.fori_loop(1, tg - 1, step_far, 0)
-    project_far(tg - 1)
+    lax.fori_loop(1, tg - 2, step_far, 0)
+    for h in range(max(tg - 2, 1), tg):
+        project_far(h)
     if wrows * hd % HD:
         lax.fori_loop(0, 4, lambda u, carry: (project(u), carry)[1], 0)
     do_ref[...] = ga_ref[...].astype(BF)
@@ -334,7 +337,7 @@
 
     lax.fori_loop(0, kv_ref.shape[0] // KB, turn, 0)
 
-    if share == 2:
+    def pair_sums():
         for d in [*range(1, ring), 0]:
             pair_copy(d).wait_recv()
             ii, kk = plane_peer(d)
@@ -349,9 +352,6 @@
             if d:
                 y_copy(d).start()
 
-    bwd_body(prompt, qb, info_ref, q_ref, kv_ref, kt_ref, o_ref, lse_ref, do_ref,
-             dq_ref, dkv_ref, qs_ref, dos_ref, del_ref, p_ref, ds_ref, dqt_ref, dk_ref, dv_ref)
-
     def dkv_copy(d, to):
         p = lax.rem(c + d, n)
         src = c if to else lax.rem(c - d + n, n)
@@ -362,8 +362,23 @@
         src = i if to else lax.rem(i - d + hd, hd)
         return remote(dq_ref.at[span(ii, tok), :], dqout_ref.at[:, span(src, G * HD)], dq_sem, d, (t, ii, k))
 
-    for d in range(1, n):
-        dkv_copy(d, True).start()
+    def backward(late, between):
+        bwd_body(late, between, prompt, qb, info_ref, q_ref, kv_ref, kt_ref, o_ref, lse_ref, do_ref,
+                 dq_ref, dkv_ref, qs_ref, dos_ref, del_ref, p_ref, ds_ref, dqt_ref, dk_ref, dv_ref)
+
+    def push(late):
+        for d in range(1, n):
+            @pl.when((lax.rem(c + d, n) * tok >= prompt) == late)
+            def _():
+                dkv_copy(d, True).start()
+
+    dk_ref[...] = jnp.zeros_like(dk_ref)
+    dv_ref[...] = jnp.zeros_like(dv_ref)
+    dqt_ref[...] = jnp.zeros_like(dqt_ref)
+    backward(False, pair_sums if share == 2 else None)
+    push(False)
+    backward(True, None)
+    push(True)
     for d in range(1, hd):
         dq_copy(d, True).start()
     own = [
@@ -464,13 +479,11 @@
     lax.fori_loop(0, blocks, query_block, 0)
 
 
-def bwd_body(prompt, qb, info_ref, q_ref, kv_ref, kt_ref, o_ref, lse_ref, do_ref,
+def bwd_body(late, between, prompt, qb, info_ref, q_ref, kv_ref, kt_ref, o_ref, lse_ref, do_ref,
                dq_ref, dkv_ref, qs_ref, dos_ref, del_ref, p_ref, ds_ref, dqt_ref, dk_ref, dv_ref):
     info = read_info(info_ref)
     first_row = lax.axis_index("tg").astype(jnp.int32) * q_ref.shape[0]
     blocks = q_ref.shape[0] // qb
-    dk_ref[...] = jnp.zeros_like(dk_ref)
-    dv_ref[...] = jnp.zeros_like(dv_ref)
 
     def query_block(i, carry):
         rows = pl.ds(pl.multiple_of(i * qb, qb), qb)
@@ -482,7 +495,6 @@
             dos_ref[h * qb:(h + 1) * qb, :] = do
             prod = do.astype(jnp.float32) * o_ref[rows, cols].astype(jnp.float32)
             del_ref[h:h + 1, :] = jnp.sum(prod.T, axis=0, keepdims=True)
-        dqt_ref[...] = jnp.zeros_like(dqt_ref)
         full, last = block_range(q_first, qb, prompt)
 
         def key_block(masked, b, carry):
@@ -505,20 +517,26 @@
                 part = slice(h * qb, (h + 1) * qb)
                 dv += dot(p_ref[h], dos_ref[part, :])
                 dk += dot(ds_ref[h], qs_ref[part, :])
-                dqt_ref[h] += dot(kt_ref[:, keys], ds_ref[h])
+                dqt_ref[i, h] += dot(kt_ref[:, keys], ds_ref[h])
             dv_ref[keys, :] += dv
             dk_ref[keys, :] += dk
             return carry
 
-        lax.fori_loop(0, full, functools.partial(key_block, False), 0)
-        lax.fori_loop(full, last, functools.partial(key_block, True), 0)
-        for h in range(G):
-            dq_ref[rows, h * HD:(h + 1) * HD] = (dqt_ref[h] * SCALE).T.astype(jnp.bfloat16)
+        if late:
+            lax.fori_loop(jnp.maximum(full, prompt // KB), last, functools.partial(key_block, True), 0)
+            for h in range(G):
+                dq_ref[rows, h * HD:(h + 1) * HD] = (dqt_ref[i, h] * SCALE).T.astype(jnp.bfloat16)
+        else:
+            lax.fori_loop(0, full, functools.partial(key_block, False), 0)
+            lax.fori_loop(full, jnp.minimum(last, prompt // KB), functools.partial(key_block, True), 0)
+        if between is not None:
+            pl.when(i == 0)(between)
         return carry
 
     lax.fori_loop(0, blocks, query_block, 0)
-    dkv_ref[:, :HD] = (dk_ref[...] * SCALE).astype(jnp.bfloat16)
-    dkv_ref[:, HD:] = dv_ref[...].astype(jnp.bfloat16)
+    half = slice(prompt, None) if late else slice(0, prompt)
+    dkv_ref[half, :HD] = (dk_ref[half, :] * SCALE).astype(jnp.bfloat16)
+    dkv_ref[half, HD:] = dv_ref[half, :].astype(jnp.bfloat16)
 
 
 VM = pl.BlockSpec(memory_space=pltpu.VMEM)
@@ -597,7 +615,7 @@
             pltpu.VMEM((8, qb), F32),
             pltpu.VMEM((G, KB, qb), BF),
             pltpu.VMEM((G, KB, qb), BF),
-            pltpu.VMEM((G, HD, qb), F32),
+            pltpu.VMEM((rows // qb, G, HD, qb), F32),
             pltpu.VMEM((keys, HD), F32),
             pltpu.VMEM((keys, HD), F32),
             dma(ring), dma(ring), dma(hd), dma(n),

time: 258 us -> 260 us (level)
  no operation moved by 1% of the time
where the time goes in v4:
time: 260 us; the launch traced here: 258 us
  Pallas kernels  249 us (96%)
  local copies, waits for them, and re-layouts  8.04 us (3%)
    pallas_call x1, Pallas kernels, gather_and_forward(): pl.pallas_call(functools.partial(gather_kernel, prompt, qb), out_shape=(s...  162 us
    pallas_call x1, Pallas kernels, backward_and_scatter(): pl.pallas_call(functools.partial(scatter_kernel, prompt, qb), out_shape=(...  86.5 us
    unnamed x11, local copies, waits for them, and re-layouts  5.42 us

profile of v4, /device:TPU:1, one launch (start us, length us, event | category | flops | bytes accessed | tf_op | source)
XLA Modules:
  0.0 258.2 jit_solution(2470796977686618773)
XLA Ops:
  0.6 0.7 slice_bitcast_fusion
  1.3 0.2 reduce-window.9
  1.5 0.6 pad_add_fusion.info_ref
  2.1 1.0 reshape.46
  3.0 1.0 reshape.47
  4.0 0.2 pad_maximum_fusion
  4.2 0.8 copy.10
  5.0 162.0 %gather_and_forward.1 = (bf16[3072,256]{1,0:T(8,128)(2,1)}, bf16[768,640]{1,0:T(8,128)(2,1)}, bf16[768,640]{1,0:T(8,128)(2,1)}, f32[3,8,256]{2,1,0:T(8,128)}, bf...) custom-call(s32[4]{0:T(128)} %pad_add_fusion.info_ref, bf16[192,1024]{1,0:T(8,128)(2,1)} %bitcast.8, ...), custom_call_target="tpu_custom_call" | custom-call | flops 6039797760 | bytes 33554432 | tf_op jit(solution)/shard_map/gather_and_forward/pallas_call | solution.py:559
  167.1 86.5 %backward_and_scatter.1 = (bf16[192,2560]{1,0:T(8,128)(2,1)}, bf16[192,2560]{1,0:T(8,128)(2,1)}, bf16[192,512]{1,0:T(8,128)(2,1)}, bf16[192,512]{1,0:T(8,128)(2,1)}) custom-call(s32[4]{0:T(128)} %pad_add_fusion.info_ref, bf16[768,5120]{1,0:T(8,128)(2,1)} %get-tuple-element.10.y_ref, bf16[768,640]{1,0:T(8,128)(2,1)} %get-tuple-element.11.q_ref, ...), custom_call_target="tpu_custom_call" | custom-call | flops 15099494400 | bytes 33554432 | tf_op jit(solution)/shard_map/backward_and_scatter/pallas_call | solution.py:596
  253.6 0.0 copy-start
  253.6 0.0 copy-start.2
  253.6 2.3 copy.15
  255.9 0.0 copy-done
  255.9 0.0 copy-start.1
  255.9 0.9 copy.16
  256.9 0.0 copy-done.2
  256.9 0.7 copy.17
  257.5 0.0 copy-done.1
  257.5 0.7 copy.18
  (1 shorter events, 0.0 us)
Async XLA Ops:
  253.6 2.3 copy-start
  253.6 3.3 %copy-start.2 = (bf16[192,512]{1,0:T(8,128)(2,1)S(1)}, bf16[192,512]{1,0:T(8,128)(2,1)}, u32[]{:S(2)}) copy-start(bf16[192,512]{1,0:T(8,128)(2,1)} %get-tuple-element.22) | copy-start | bytes 589828
  255.9 1.6 copy-start.1

commit v5 on v3

--- a/solution.py
+++ b/solution.py
@@ -243,9 +243,8 @@
         return carry
 
     lax.fori_loop(0, kvall_ref.shape[0] // KB, turn, 0)
-    blocks = o_ref.shape[0] // qb
     fwd_body(prompt, qb, info_ref, qall_ref, kvall_ref, vt_ref, o_ref, lse_ref, m_ref, l_ref, acc_ref,
-             arrive_first, max(blocks - 2, 0))
+             arrive_first, 0)
 
     for d in range(1, ring):
         g_copy(d, False).wait_recv()

time: 258 us -> 257 us (level)
  no operation moved by 1% of the time
where the time goes in v5:
time: 257 us
  Pallas kernels  247 us (96%)
  local copies, waits for them, and re-layouts  8.04 us (3%)
    pallas_call x1, Pallas kernels, gather_and_forward(): pl.pallas_call(functools.partial(gather_kernel, prompt, qb), out_shape=(s...  160 us
    pallas_call x1, Pallas kernels, backward_and_scatter(): pl.pallas_call(functools.partial(scatter_kernel, prompt, qb), out_shape=(...  87.3 us
    unnamed x11, local copies, waits for them, and re-layouts  5.42 us

profile of v5, /device:TPU:1, one launch (start us, length us, event | category | flops | bytes accessed | tf_op | source)
XLA Modules:
  0.0 256.7 jit_solution(14753715424603652337)
XLA Ops:
  0.6 0.7 slice_bitcast_fusion
  1.3 0.2 reduce-window.9
  1.5 0.6 pad_add_fusion.info_ref
  2.1 1.0 reshape.46
  3.0 1.0 reshape.47
  4.0 0.2 pad_maximum_fusion
  4.2 0.8 copy.10
  5.0 159.6 %gather_and_forward.1 = (bf16[3072,256]{1,0:T(8,128)(2,1)}, bf16[768,640]{1,0:T(8,128)(2,1)}, bf16[768,640]{1,0:T(8,128)(2,1)}, f32[3,8,256]{2,1,0:T(8,128)}, bf...) custom-call(s32[4]{0:T(128)} %pad_add_fusion.info_ref, bf16[192,1024]{1,0:T(8,128)(2,1)} %bitcast.8, ...), custom_call_target="tpu_custom_call" | custom-call | flops 6039797760 | bytes 33554432 | tf_op jit(solution)/shard_map/gather_and_forward/pallas_call | solution.py:540
  164.7 87.3 %backward_and_scatter.1 = (bf16[192,2560]{1,0:T(8,128)(2,1)}, bf16[192,2560]{1,0:T(8,128)(2,1)}, bf16[192,512]{1,0:T(8,128)(2,1)}, bf16[192,512]{1,0:T(8,128)(2,1)}) custom-call(s32[4]{0:T(128)} %pad_add_fusion.info_ref, bf16[768,5120]{1,0:T(8,128)(2,1)} %get-tuple-element.10.y_ref, bf16[768,640]{1,0:T(8,128)(2,1)} %get-tuple-element.11.q_ref, ...), custom_call_target="tpu_custom_call" | custom-call | flops 15099494400 | bytes 33554432 | tf_op jit(solution)/shard_map/backward_and_scatter/pallas_call | solution.py:577
  252.0 0.0 copy-start
  252.1 0.0 copy-start.2
  252.1 2.3 copy.15
  254.4 0.0 copy-done
  254.4 0.0 copy-start.1
  254.4 0.9 copy.16
  255.3 0.0 copy-done.2
  255.3 0.7 copy.17
  256.0 0.0 copy-done.1
  256.0 0.7 copy.18
  (1 shorter events, 0.0 us)
Async XLA Ops:
  252.0 2.3 copy-start
  252.1 3.3 %copy-start.2 = (bf16[192,512]{1,0:T(8,128)(2,1)S(1)}, bf16[192,512]{1,0:T(8,128)(2,1)}, u32[]{:S(2)}) copy-start(bf16[192,512]{1,0:T(8,128)(2,1)} %get-tuple-element.22) | copy-start | bytes 589828
  254.4 1.6 copy-start.1
